TPU v7x, 32 devices: a whole 2x2x4 slice. The times are simulated.
32 devices in a mesh: dp: 8 (over z, x), seq: 4 (over y, core).
Axes of the slice: x: 2, y: 2, z: 4, core: 2. Of those that a mesh axis runs over, the one named last changes fastest.
Arguments:
- hidden_in: bfloat16 [16, 1024, 768], P('dp', 'seq'), may hold values from -6 to 6
- passage_lengths: int32 [16, 8], P('dp'), may hold values from 0 to 512, as said below
- w_qkv: bfloat16 [768, 2304], replicated, may hold values from -0.3125 to 0.3125
- b_query: bfloat16 [768], replicated, may hold values from -3 to 3
- b_value: bfloat16 [768], replicated, may hold values from -3 to 3
- w_attn_out: bfloat16 [768, 768], replicated, may hold values from -0.875 to 0.875
- b_attn_out: bfloat16 [768], replicated, may hold values from -3 to 3
- gain_attn: bfloat16 [768], replicated, may hold values from 0.5 to 1.5
- bias_attn: bfloat16 [768], replicated, may hold values from -3 to 3
- w_inner: bfloat16 [768, 3072], replicated, may hold values from -0.21875 to 0.21875
- b_inner: bfloat16 [3072], replicated, may hold values from -3 to 3
- w_outer: bfloat16 [3072, 768], replicated, may hold values from -0.15625 to 0.15625
- b_outer: bfloat16 [768], replicated, may hold values from -3 to 3
- gain_ffn: bfloat16 [768], replicated, may hold values from 0.5 to 1.5
- bias_ffn: bfloat16 [768], replicated, may hold values from -3 to 3
- grad_out: bfloat16 [16, 1024, 768], P('dp', 'seq'), may hold values from -6 to 6
Outputs:
- out: float32 [16, 1024, 768], P('dp', 'seq')
- pooled: float32 [16, 8, 768], P('dp')
- grad_in: float32 [16, 1024, 768], P('dp', 'seq')
- grad_w_qkv: float32 [768, 2304], P('dp')
- grad_b_query: float32 [768], P('dp')
- grad_b_value: float32 [768], P('dp')
- grad_w_attn_out: float32 [768, 768], P('dp')
- grad_b_attn_out: float32 [768], P('dp')
- grad_gain_attn: float32 [768], P('dp')
- grad_bias_attn: float32 [768], P('dp')
- grad_w_inner: float32 [768, 3072], P('dp')
- grad_b_inner: float32 [3072], P('dp')
- grad_w_outer: float32 [3072, 768], P('dp')
- grad_b_outer: float32 [768], P('dp')
- grad_gain_ffn: float32 [768], P('dp')
- grad_bias_ffn: float32 [768], P('dp')
Inputs may be any that keep to these rules, and one draw needn't show every extreme that they name: `passage_lengths`: each row lists its passages' lengths in order, each 20 or more, then zeros; a row's lengths sum to at most 1024, and its later positions are padding.
All inputs are finite; a program needn't handle non-finite values.
Results may differ from a plain program's by a relative error of at most 0.02.
Values may be sent and summed in bfloat16 or wider, within the bound.
No kernel may reach another device: no remote copies, remote signals or barrier semaphores. Data moves between devices by JAX's collectives and lax.ppermute only.
A program may use at most 192 MiB of HBM per device.

v0:
```python
import jax
import jax.numpy as jnp
from jax import lax
from jax.sharding import PartitionSpec as P

HEADS = 12


PRECISE = lax.Precision.HIGHEST


def layer_norm(inputs, gain_vec, shift_vec):
    centre = inputs - jnp.mean(inputs, axis=-1, keepdims=True)
    spread = jnp.mean(centre * centre, axis=-1, keepdims=True)
    return centre * lax.rsqrt(spread + 1e-12) * gain_vec + shift_vec


def gelu_exact(inputs):
    return jax.nn.gelu(inputs, approximate=False)


def product(left, right):
    return jnp.dot(left, right, preferred_element_type=jnp.float32)


def transposed(left, right):
    return lax.dot_general(
        left, right, (((0,), (0,)), ((), ())), preferred_element_type=jnp.float32
    )


def back_product(left, right):
    return lax.dot_general(
        left, right, (((1,), (1,)), ((), ())), preferred_element_type=jnp.float32
    )


def column_sum(values):
    return jnp.sum(values.astype(jnp.float32), axis=0)


def split_heads(values):
    return values.reshape(values.shape[0], HEADS, values.shape[1] // HEADS)


def head_scale(values):
    return (values.shape[1] // HEADS) ** (-0.5)


def masked_scores(queries, keys_in, seg_query, seg_key):
    raw_scores = jnp.einsum(
        "qhd,khd->hqk",
        split_heads(queries),
        split_heads(keys_in),
        preferred_element_type=jnp.float32,
    )
    raw_scores = raw_scores * head_scale(queries)
    same_seg = seg_query[:, None] == seg_key[None, :]
    return jnp.where(same_seg[None], raw_scores, -1e30)


def score_grads(
    queries, keys_in, values_in, grads_in, seg_query, seg_key, row_max, row_total, centre
):
    scores = masked_scores(queries, keys_in, seg_query, seg_key)
    prob_full = jnp.exp(scores - row_max[:, :, None]) / row_total[:, :, None]
    grad_probs = jnp.einsum(
        "qhd,khd->hqk",
        split_heads(grads_in),
        split_heads(values_in),
        preferred_element_type=jnp.float32,
    )
    centre = jnp.sum(prob_full * grad_probs, axis=2)
    d_scores = (prob_full * (grad_probs - centre[:, :, None])).astype(jnp.bfloat16)
    return (prob_full, d_scores, centre)


def key_side(queries, grads_in, keys_in, prob_full, d_scores):
    d_key = jnp.einsum(
        "hqk,qhd->khd", d_scores, split_heads(queries), preferred_element_type=jnp.float32
    ) * head_scale(queries)
    d_value = jnp.einsum(
        "hqk,qhd->khd",
        prob_full.astype(jnp.bfloat16),
        split_heads(grads_in),
        preferred_element_type=jnp.float32,
    )
    return (d_key.reshape(keys_in.shape), d_value.reshape(keys_in.shape))


def attend_row(pieces):
    queries, keys_in, values_in, seg_query, seg_key = pieces
    scores = masked_scores(queries, keys_in, seg_query, seg_key)
    row_max = jnp.max(scores, axis=2, keepdims=True)
    exp_scores = jnp.exp(scores - row_max)
    row_total = jnp.sum(exp_scores, axis=2, keepdims=True)
    prob_low = (exp_scores / row_total).astype(jnp.bfloat16)
    mixed = jnp.einsum(
        "hqk,khd->qhd", prob_low, split_heads(values_in), preferred_element_type=jnp.float32
    )
    return (mixed.reshape(queries.shape).astype(jnp.bfloat16), row_max[:, :, 0], row_total[:, :, 0])


def query_back_full(pieces):
    queries, keys_in, values_in, grads_in, seg_query, seg_key, row_max, row_total = pieces
    prob_full, d_scores, centre = score_grads(
        queries, keys_in, values_in, grads_in, seg_query, seg_key, row_max, row_total, None
    )
    d_query = jnp.einsum(
        "hqk,khd->qhd", d_scores, split_heads(keys_in), preferred_element_type=jnp.float32
    ) * head_scale(queries)
    d_key, d_value = key_side(queries, grads_in, keys_in, prob_full, d_scores)
    return (d_query.reshape(queries.shape).astype(jnp.bfloat16), centre, d_key, d_value)


def body(
    hidden_in,
    passage_lengths,
    w_qkv,
    b_query,
    b_value,
    w_attn_out,
    b_attn_out,
    gain_attn,
    bias_attn,
    w_inner,
    b_inner,
    w_outer,
    b_outer,
    gain_ffn,
    bias_ffn,
    grad_out,
):
    row_count, shard_len, model_dim = hidden_in.shape
    full_len = shard_len * lax.axis_size("seq")
    token_count = row_count * shard_len
    row_shape = (row_count, shard_len, model_dim)
    pass_ends = jnp.cumsum(passage_lengths, axis=1, dtype=jnp.int32)
    positions = jnp.arange(full_len, dtype=jnp.int32)
    seg_full = jnp.sum(
        (positions[None, :, None] >= pass_ends[:, None, :]).astype(jnp.int32),
        axis=2,
        dtype=jnp.int32,
    )
    seg_local = lax.dynamic_slice_in_dim(seg_full, lax.axis_index("seq") * shard_len, shard_len, 1)
    hidden_flat = hidden_in.reshape(token_count, model_dim)
    packed = product(hidden_flat, w_qkv)
    query_rows = (packed[:, :model_dim] + b_query).astype(jnp.bfloat16).reshape(row_shape)
    key_rows = packed[:, model_dim : 2 * model_dim].astype(jnp.bfloat16).reshape(row_shape)
    value_rows = (packed[:, 2 * model_dim :] + b_value).astype(jnp.bfloat16).reshape(row_shape)
    key_full, value_full = (
        lax.all_gather(key_rows, "seq", axis=1, tiled=True),
        lax.all_gather(value_rows, "seq", axis=1, tiled=True),
    )
    mixed_rows, row_maxes, row_totals = lax.map(
        attend_row, (query_rows, key_full, value_full, seg_local, seg_full)
    )
    mixed_flat = mixed_rows.reshape(token_count, model_dim)
    branch = product(mixed_flat, w_attn_out) + b_attn_out
    norm_first, norm_one_back = jax.vjp(
        layer_norm,
        hidden_flat.astype(jnp.float32) + branch,
        gain_attn.astype(jnp.float32),
        bias_attn.astype(jnp.float32),
    )
    first_low = norm_first.astype(jnp.bfloat16)
    inner_pre = product(first_low, w_inner) + b_inner
    active, gelu_back = jax.vjp(gelu_exact, inner_pre)
    active_low = active.astype(jnp.bfloat16)
    second = product(active_low, w_outer) + b_outer
    output, norm_two_back = jax.vjp(
        layer_norm, norm_first + second, gain_ffn.astype(jnp.float32), bias_ffn.astype(jnp.float32)
    )
    slot_count = passage_lengths.shape[1]
    onehot = (
        seg_local[:, None, :] == jnp.arange(slot_count, dtype=jnp.int32)[None, :, None]
    ).astype(jnp.float32)
    partial_value = jnp.einsum("rsc,rcd->rsd", onehot, output.reshape(row_shape), precision=PRECISE)
    summed = lax.psum(partial_value.astype(jnp.bfloat16), "seq").astype(jnp.float32)
    pooled = summed / jnp.maximum(passage_lengths.astype(jnp.float32), 1.0)[:, :, None]
    cotangent = grad_out.reshape(token_count, model_dim).astype(jnp.float32)
    d_sum_two, grad_gain_ffn, grad_bias_ffn = norm_two_back(cotangent)
    d_second = d_sum_two.astype(jnp.bfloat16)
    grad_b_outer = column_sum(d_second)
    grad_w_outer = transposed(active_low, d_second)
    d_inner = gelu_back(back_product(d_second, w_outer))[0].astype(jnp.bfloat16)
    grad_b_inner = column_sum(d_inner)
    grad_w_inner = transposed(first_low, d_inner)
    d_first = d_sum_two + back_product(d_inner, w_inner)
    d_sum_one, grad_gain_attn, grad_bias_attn = norm_one_back(d_first)
    d_branch = d_sum_one.astype(jnp.bfloat16)
    grad_b_attn_out = column_sum(d_branch)
    grad_w_attn_out = transposed(mixed_flat, d_branch)
    grad_rows = back_product(d_branch, w_attn_out).astype(jnp.bfloat16).reshape(row_shape)
    key_back, value_back = (
        lax.all_gather(key_rows, "seq", axis=1, tiled=True),
        lax.all_gather(value_rows, "seq", axis=1, tiled=True),
    )
    query_pieces = (
        query_rows,
        key_back,
        value_back,
        grad_rows,
        seg_local,
        seg_full,
        row_maxes,
        row_totals,
    )
    d_query, centres, key_part, value_part = lax.map(query_back_full, query_pieces)
    key_grad, value_grad = (
        lax.psum_scatter(
            key_part.astype(jnp.bfloat16), "seq", scatter_dimension=1, tiled=True
        ).astype(jnp.float32),
        lax.psum_scatter(
            value_part.astype(jnp.bfloat16), "seq", scatter_dimension=1, tiled=True
        ).astype(jnp.float32),
    )
    d_query_flat = d_query.reshape(token_count, model_dim)
    d_key_low = key_grad.astype(jnp.bfloat16).reshape(token_count, model_dim)
    d_value_low = value_grad.astype(jnp.bfloat16).reshape(token_count, model_dim)
    d_packed = jnp.concatenate((d_query_flat, d_key_low, d_value_low), axis=1)
    grad_w_qkv = transposed(hidden_flat, d_packed)
    grad_b_query = column_sum(d_query_flat)
    grad_b_value = column_sum(d_value_low)
    grad_in = d_sum_one + back_product(d_packed, w_qkv)
    (
        sum_w_qkv,
        sum_b_query,
        sum_b_value,
        sum_w_attn_out,
        sum_b_attn_out,
        sum_gain_attn,
        sum_bias_attn,
        sum_w_inner,
        sum_b_inner,
        sum_w_outer,
        sum_b_outer,
        sum_gain_ffn,
        sum_bias_ffn,
    ) = (
        lax.psum_scatter(
            grad_w_qkv.astype(jnp.bfloat16), "dp", scatter_dimension=0, tiled=True
        ).astype(jnp.float32),
        lax.psum_scatter(
            grad_b_query.astype(jnp.bfloat16), "dp", scatter_dimension=0, tiled=True
        ).astype(jnp.float32),
        lax.psum_scatter(
            grad_b_value.astype(jnp.bfloat16), "dp", scatter_dimension=0, tiled=True
        ).astype(jnp.float32),
        lax.psum_scatter(
            grad_w_attn_out.astype(jnp.bfloat16), "dp", scatter_dimension=0, tiled=True
        ).astype(jnp.float32),
        lax.psum_scatter(
            grad_b_attn_out.astype(jnp.bfloat16), "dp", scatter_dimension=0, tiled=True
        ).astype(jnp.float32),
        lax.psum_scatter(
            grad_gain_attn.astype(jnp.bfloat16), "dp", scatter_dimension=0, tiled=True
        ).astype(jnp.float32),
        lax.psum_scatter(
            grad_bias_attn.astype(jnp.bfloat16), "dp", scatter_dimension=0, tiled=True
        ).astype(jnp.float32),
        lax.psum_scatter(
            grad_w_inner.astype(jnp.bfloat16), "dp", scatter_dimension=0, tiled=True
        ).astype(jnp.float32),
        lax.psum_scatter(
            grad_b_inner.astype(jnp.bfloat16), "dp", scatter_dimension=0, tiled=True
        ).astype(jnp.float32),
        lax.psum_scatter(
            grad_w_outer.astype(jnp.bfloat16), "dp", scatter_dimension=0, tiled=True
        ).astype(jnp.float32),
        lax.psum_scatter(
            grad_b_outer.astype(jnp.bfloat16), "dp", scatter_dimension=0, tiled=True
        ).astype(jnp.float32),
        lax.psum_scatter(
            grad_gain_ffn.astype(jnp.bfloat16), "dp", scatter_dimension=0, tiled=True
        ).astype(jnp.float32),
        lax.psum_scatter(
            grad_bias_ffn.astype(jnp.bfloat16), "dp", scatter_dimension=0, tiled=True
        ).astype(jnp.float32),
    )
    (
        tot_w_qkv,
        tot_b_query,
        tot_b_value,
        tot_w_attn_out,
        tot_b_attn_out,
        tot_gain_attn,
        tot_bias_attn,
        tot_w_inner,
        tot_b_inner,
        tot_w_outer,
        tot_b_outer,
        tot_gain_ffn,
        tot_bias_ffn,
    ) = (
        lax.psum(sum_w_qkv.astype(jnp.bfloat16), "seq").astype(jnp.float32),
        lax.psum(sum_b_query.astype(jnp.bfloat16), "seq").astype(jnp.float32),
        lax.psum(sum_b_value.astype(jnp.bfloat16), "seq").astype(jnp.float32),
        lax.psum(sum_w_attn_out.astype(jnp.bfloat16), "seq").astype(jnp.float32),
        lax.psum(sum_b_attn_out.astype(jnp.bfloat16), "seq").astype(jnp.float32),
        lax.psum(sum_gain_attn.astype(jnp.bfloat16), "seq").astype(jnp.float32),
        lax.psum(sum_bias_attn.astype(jnp.bfloat16), "seq").astype(jnp.float32),
        lax.psum(sum_w_inner.astype(jnp.bfloat16), "seq").astype(jnp.float32),
        lax.psum(sum_b_inner.astype(jnp.bfloat16), "seq").astype(jnp.float32),
        lax.psum(sum_w_outer.astype(jnp.bfloat16), "seq").astype(jnp.float32),
        lax.psum(sum_b_outer.astype(jnp.bfloat16), "seq").astype(jnp.float32),
        lax.psum(sum_gain_ffn.astype(jnp.bfloat16), "seq").astype(jnp.float32),
        lax.psum(sum_bias_ffn.astype(jnp.bfloat16), "seq").astype(jnp.float32),
    )
    return (
        output.reshape(row_shape),
        pooled,
        grad_in.reshape(row_shape),
        tot_w_qkv,
        tot_b_query,
        tot_b_value,
        tot_w_attn_out,
        tot_b_attn_out,
        tot_gain_attn,
        tot_bias_attn,
        tot_w_inner,
        tot_b_inner,
        tot_w_outer,
        tot_b_outer,
        tot_gain_ffn,
        tot_bias_ffn,
    )


def solution(mesh):
    placed = (
        P("dp", "seq", None),
        P("dp", None),
        P(),
        P(),
        P(),
        P(),
        P(),
        P(),
        P(),
        P(),
        P(),
        P(),
        P(),
        P(),
        P(),
        P("dp", "seq", None),
    )
    return jax.shard_map(
        body,
        mesh=mesh,
        in_specs=placed,
        out_specs=(
            P("dp", "seq", None),
            P("dp", None, None),
            P("dp", "seq", None),
            P("dp", None),
            P("dp"),
            P("dp"),
            P("dp", None),
            P("dp"),
            P("dp"),
            P("dp"),
            P("dp", None),
            P("dp"),
            P("dp", None),
            P("dp"),
            P("dp"),
            P("dp"),
        ),
        check_vma=False,
    )
```

profile of v0, /device:TPU:0, one launch (start us, length us, event | category | flops | bytes accessed | tf_op | source)
XLA Modules:
  0.0 813.7 jit_solution(7223869876091820357)
XLA Ops:
  33.5 16.5 %all-gather.3.cloned.1.call-done = bf16[2,1024,768]{1,2,0:T(8,128)(2,1)} async-done(((bf16[2,256,768]{1,2,0:T(8,128)(2,1)}), bf16[2,1024,768]{1,2,0:T(8,128)(2,1)}) %all-gather.3.cloned.1.call-update) | async-done | bytes 3145744 | tf_op jit(solution)/shard_map/all_gather | solution.py:153
  50.0 31.1 %all-gather.5.cloned.1.call-done = bf16[2,1024,768]{1,2,0:T(8,128)(2,1)} async-done(((bf16[2,256,768]{1,2,0:T(8,128)(2,1)}), bf16[2,1024,768]{1,2,0:T(8,128)(2,1)}) %all-gather.5.cloned.1.call-update) | async-done | bytes 3145744 | tf_op jit(solution)/shard_map/all_gather | solution.py:152
  81.1 33.8 %while.28 = (s32[]{:T(128)}, bf16[2,256,768]{2,1,0:T(8,128)(2,1)}, f32[2,12,256]{2,1,0:T(8,128)}, f32[2,12,256]{2,1,0:T(8,128)}, bf16[2,1024,768]{1,2,0:T(8,128)...) while((s32[]{:T(128)}, bf16[2,256,768]{2,1,0:T(8,128)(2,1)}, ...), condition=%wide.region_5.6_spmd, body=%wide.region_2.5_spmd.sunk | while | flops 843507712 | bytes 67645232 | solution.py:155
  118.1 19.8 %multiply_convert_fusion.1 = (bf16[512,3072]{1,0:T(8,128)(2,1)S(1)}, f32[512,3072]{1,0:T(8,128)}, f32[512,3072]{1,0:T(8,128)}) fusion(f32[3072]{0:T(1024)S(1)} %copy-done.30, bf16[768,3072]{1,0:T(8,128)(2,1)} %param.29, f32[512,768]{1,0:T(8,128)S(1)} %get-tuple-element.379, f32[768]{0:T(1024)S(1)} %copy-done.38, f32[768]{0:T(1024)S(1)} %convert_element_type.233, ...), kind=kOutput, calls=%fused_computation.41 | convolution fusion | flops 2521694208 | bytes 22042624 | tf_op jit(solution)/shard_map/dot_general | solution.py:23
  145.1 9.8 %fusion.32 = (bf16[3072]{0:T(1024)(128)(2,1)}, bf16[512,3072]{1,0:T(8,128)(2,1)}) fusion(f32[512,3072]{1,0:T(8,128)} %get-tuple-element.364, f32[512,3072]{1,0:T(8,128)} %get-tuple-element.380, f32[3072]{0:T(1024)S(1)} %copy-done.30, bf16[512,768]{1,0:T(8,128)(2,1)S(1)} %get-tuple-element.354, bf16[3072,768]{1,0:T(8,128)(2,1)S(1)} %bitcast.172), kind=kOutput, calls=%fused_computation.110 | convolution fusion | flops 2441081856 | bytes 21252096 | tf_op jit(solution)/shard_map/dot_general | solution.py:33
  165.8 118.4 %while.29 = (s32[]{:T(128)}, bf16[2,256,768]{1,2,0:T(8,128)(2,1)}, bf16[2,1024,768]{2,1,0:T(8,128)(2,1)}, bf16[2,1024,768]{2,1,0:T(8,128)(2,1)}, bf16[2,1024,768...) while((s32[]{:T(128)}, bf16[2,256,768]{1,2,0:T(8,128)(2,1)}, ...), condition=%wide.region_17.18_spmd, body=%wide.region_15.17_spmd.sunk | while | flops 2046948352 | bytes 229294544 | solution.py:209
  172.8 8.0 fusion.109
  181.1 8.3 %multiply_reduce_fusion.6 = (f32[12,256]{1,0:T(8,128)S(1)}, f32[12,256,1024]{2,1,0:T(8,128)S(1)}) fusion(f32[12,256,1024]{2,1,0:T(8,128)} %fusion.109, f32[12,256]{1,0:T(8,128)S(1)} %get-tuple-element.528, f32[12,256]{1,0:T(8,128)S(1)} %get-tuple-element.529, bf16[256,12,64]{0,2,1:T(8,128)(2,1)S(1)} %bitcast.151, ...), kind=kOutput, calls=%fused_computation.19.clone.1 | convolution fusion | flops 421524480 | bytes 27430912 | tf_op jit(solution)/shard_map/while/body/eval_jaxpr/qhd,khd->hqk/dot_general | solution.py:51
  189.4 9.6 %multiply_convert_fusion.3 = bf16[12,256,1024]{2,1,0:T(8,128)(2,1)S(1)} fusion(f32[12,256,1024]{2,1,0:T(8,128)S(1)} %get-tuple-element.530, f32[12,256,1024]{2,1,0:T(8,128)} %fusion.109, f32[12,256]{1,0:T(8,128)S(1)} %get-tuple-element.531), kind=kLoop, calls=%fused_computation.18.clone.1 | loop fusion | flops 9437184 | bytes 31469568 | tf_op jit(solution)/shard_map/while/body/eval_jaxpr/convert_element_type | solution.py:74
  212.5 7.3 fusion.111
  231.8 8.0 fusion.109
  240.1 8.3 %multiply_reduce_fusion.6 = (f32[12,256]{1,0:T(8,128)S(1)}, f32[12,256,1024]{2,1,0:T(8,128)S(1)}) fusion(f32[12,256,1024]{2,1,0:T(8,128)} %fusion.109, f32[12,256]{1,0:T(8,128)S(1)} %get-tuple-element.528, f32[12,256]{1,0:T(8,128)S(1)} %get-tuple-element.529, bf16[256,12,64]{0,2,1:T(8,128)(2,1)S(1)} %bitcast.151, ...), kind=kOutput, calls=%fused_computation.19.clone.1 | convolution fusion | flops 421524480 | bytes 27430912 | tf_op jit(solution)/shard_map/while/body/eval_jaxpr/qhd,khd->hqk/dot_general | solution.py:51
  248.4 9.6 %multiply_convert_fusion.3 = bf16[12,256,1024]{2,1,0:T(8,128)(2,1)S(1)} fusion(f32[12,256,1024]{2,1,0:T(8,128)S(1)} %get-tuple-element.530, f32[12,256,1024]{2,1,0:T(8,128)} %fusion.109, f32[12,256]{1,0:T(8,128)S(1)} %get-tuple-element.531), kind=kLoop, calls=%fused_computation.18.clone.1 | loop fusion | flops 9437184 | bytes 31469568 | tf_op jit(solution)/shard_map/while/body/eval_jaxpr/convert_element_type | solution.py:74
  271.6 7.3 fusion.111
  287.1 35.2 %reduce-scatter.9.cloned.1.call-done = bf16[2,256,768]{2,1,0:T(8,128)(2,1)} async-done(((bf16[2,1024,768]{2,1,0:T(8,128)(2,1)}), bf16[2,256,768]{2,1,0:T(8,128)(2,1)}) %reduce-scatter.9.cloned.1.call-update) | async-done | bytes 786448 | tf_op jit(solution)/shard_map/reduce_scatter | solution.py:211
  322.3 40.5 %reduce-scatter.11.cloned.1.call-done = bf16[2,256,768]{2,1,0:T(8,128)(2,1)} async-done(((bf16[2,1024,768]{2,1,0:T(8,128)(2,1)}), bf16[2,256,768]{2,1,0:T(8,128)(2,1)}) %reduce-scatter.11.cloned.1.call-update) | async-done | bytes 786448 | tf_op jit(solution)/shard_map/reduce_scatter | solution.py:214
  377.7 6.9 convolution_convert_fusion
  385.3 7.4 convolution_convert_fusion.1
  397.8 55.8 %reduce-scatter.19.cloned.1.call-done = bf16[96,2304]{1,0:T(8,128)(2,1)} async-done(((bf16[768,2304]{1,0:T(8,128)(2,1)}), bf16[96,2304]{1,0:T(8,128)(2,1)}) %reduce-scatter.19.cloned.1.call-update) | async-done | bytes 442384
  455.6 65.4 %reduce-scatter.13.cloned.1.call-done = bf16[96,768]{1,0:T(8,128)(2,1)} async-done(((bf16[768,768]{1,0:T(8,128)(2,1)}), bf16[96,768]{1,0:T(8,128)(2,1)}) %reduce-scatter.13.cloned.1.call-update) | async-done | bytes 147472 | tf_op jit(solution)/shard_map/reduce_scatter | solution.py:250
  521.1 97.9 %reduce-scatter.17.cloned.1.call-done = bf16[384,768]{1,0:T(8,128)(2,1)} async-done(((bf16[3072,768]{1,0:T(8,128)(2,1)}), bf16[384,768]{1,0:T(8,128)(2,1)}) %reduce-scatter.17.cloned.1.call-update) | async-done | bytes 589840 | tf_op jit(solution)/shard_map/reduce_scatter | solution.py:268
  618.9 98.7 %reduce-scatter.15.cloned.1.call-done = bf16[96,3072]{1,0:T(8,128)(2,1)} async-done(((bf16[768,3072]{1,0:T(8,128)(2,1)}), bf16[96,3072]{1,0:T(8,128)(2,1)}) %reduce-scatter.15.cloned.1.call-update) | async-done | bytes 589840 | tf_op jit(solution)/shard_map/reduce_scatter | solution.py:262
  723.5 37.2 %all-reduce.9 = (bf16[768]{0:T(1024)(128)(2,1)}, bf16[768]{0:T(1024)(128)(2,1)}, bf16[768]{0:T(1024)(128)(2,1)}, bf16[768]{0:T(1024)(128)(2,1)}, bf16[768]{0:T(1...) all-reduce(bf16[768]{0:T(1024)(128)(2,1)S(1)} %reduce_sum.239, ...), channel_id=5, replica_groups=mesh['dp'=8,'seq'=4] {'dp'}, use_global_device_ids=true, to_apply=%region_23.24.clone | all-reduce | flops 9216 | bytes 36864
  770.9 11.5 %all-reduce.10 = (bf16[2,8,768]{2,1,0:T(8,128)(2,1)}, bf16[96]{0:T(256)(128)(2,1)}, bf16[96]{0:T(256)(128)(2,1)}, bf16[96]{0:T(256)(128)(2,1)}, bf16[96]{0:T(256...) all-reduce(bf16[2,8,768]{2,1,0:T(8,128)(2,1)} %convolution_convert_, ...), channel_id=1, replica_groups=mesh['dp'=8,'seq'=4] {'seq'}, use_global_device_ids=true, to_apply=%region_10.11 | all-reduce | flops 13440 | bytes 53760 | tf_op jit(solution)/shard_map/psum | solution.py:179
  (283 shorter events, 197.1 us)
Async XLA Ops:
  7.2 42.8 %all-gather.3.cloned.1.call-start = ((), (), s32[]{:S(2)}) async-start(), calls=%async_computation.6 | async-start | bytes 3932160 | tf_op jit(solution)/shard_map/all_gather | solution.py:153
  18.2 10.8 %copy-start.37 = (bf16[3072]{0:T(1024)(128)(2,1)S(1)}, bf16[3072]{0:T(1024)(128)(2,1)}, u32[]{:S(2)}) copy-start(bf16[3072]{0:T(1024)(128)(2,1)} %param.30) | copy-start | bytes 18436
  18.2 62.9 %all-gather.5.cloned.1.call-start = ((), (), s32[]{:S(2)}) async-start(), calls=%async_computation.7 | async-start | bytes 3932160 | tf_op jit(solution)/shard_map/all_gather | solution.py:152
  22.9 299.3 %reduce-scatter.9.cloned.1.call-start = ((), (), s32[]{:S(2)}) async-start(), calls=%async_computation.8 | async-start | bytes 3932160 | tf_op jit(solution)/shard_map/reduce_scatter | solution.py:211
  27.7 132.8 %copy-start.27 = (f32[768]{0:T(1024)}, f32[768]{0:T(1024)S(1)}, u32[]{:S(2)}) copy-start(f32[768]{0:T(1024)S(1)} %convert_element_type.233) | copy-start | bytes 9220
  114.9 23.0 %slice-start = ((s8[4718592]{0:T(1024)(128)(4,1)}), s8[4194304]{0:T(1024)(128)(4,1)S(1)}, s32[]{:S(2)}) async-start(s8[4718592]{0:T(1024)(128)(4,1)} %bitcast.171), calls=%async_computation.15 | async-start | bytes 8388608
  117.7 42.9 %copy-start.11 = (f32[512,768]{1,0:T(8,128)}, f32[512,768]{1,0:T(8,128)S(1)}, u32[]{:S(2)}) copy-start(f32[512,768]{1,0:T(8,128)S(1)} %get-tuple-element.379) | copy-start | bytes 4718596
  117.7 42.9 %copy-start.25 = (f32[512]{0:T(512)}, f32[512]{0:T(512)S(1)}, u32[]{:S(2)}) copy-start(f32[512]{0:T(512)S(1)} %broadcast_multiply_fusion.1) | copy-start | bytes 6148
  118.0 42.6 %copy-start.33 = (f32[512]{0:T(512)}, f32[512]{0:T(512)S(1)}, u32[]{:S(2)}) copy-start(f32[512]{0:T(512)S(1)} %fusion.24) | copy-start | bytes 6148
  118.0 19.9 %copy-start.39 = (f32[768]{0:T(1024)S(1)}, f32[768]{0:T(1024)}, u32[]{:S(2)}) copy-start(f32[768]{0:T(1024)} %convert_element_type.238) | copy-start | bytes 9220
  118.0 19.9 %slice-start.1 = ((s8[4718592]{0:T(1024)(128)(4,1)}), s8[524288]{0:T(1024)(128)(4,1)S(1)}, s32[]{:S(2)}) async-start(s8[4718592]{0:T(1024)(128)(4,1)} %bitcast.171), calls=%async_computation.16 | async-start | bytes 1048576
  142.4 12.5 %slice-start.2 = ((s8[4718592]{0:T(1024)(128)(4,1)}), s8[4194304]{0:T(1024)(128)(4,1)S(1)}, s32[]{:S(2)}) async-start(s8[4718592]{0:T(1024)(128)(4,1)} %bitcast.173), calls=%async_computation.17 | async-start | bytes 8388608
  145.1 9.8 %copy-start.16 = (bf16[512,768]{1,0:T(8,128)(2,1)}, bf16[512,768]{1,0:T(8,128)(2,1)S(1)}, u32[]{:S(2)}) copy-start(bf16[512,768]{1,0:T(8,128)(2,1)S(1)} %get-tuple-element.354) | copy-start | bytes 2359300
  145.1 9.8 %slice-start.3 = ((s8[4718592]{0:T(1024)(128)(4,1)}), s8[524288]{0:T(1024)(128)(4,1)S(1)}, s32[]{:S(2)}) async-start(s8[4718592]{0:T(1024)(128)(4,1)} %bitcast.173), calls=%async_computation.18 | async-start | bytes 1048576
  189.4 9.7 %copy-start.2 = (f32[12,256,1024]{2,1,0:T(8,128)}, f32[12,256,1024]{2,1,0:T(8,128)S(1)}, u32[]{:S(2)}) copy-start(f32[12,256,1024]{2,1,0:T(8,128)S(1)} %get-tuple-element.530) | copy-start | bytes 37748740 | tf_op jit(solution)/shard_map/while
  284.2 78.6 %reduce-scatter.11.cloned.1.call-start = ((), (), s32[]{:S(2)}) async-start(), calls=%async_computation.9 | async-start | bytes 3932160 | tf_op jit(solution)/shard_map/reduce_scatter | solution.py:214
  284.8 168.8 %reduce-scatter.19.cloned.1.call-start = ((), (), s32[]{:S(2)}) async-start(), calls=%async_computation.13 | async-start | bytes 3981312
  374.2 146.8 %reduce-scatter.13.cloned.1.call-start = ((), (), s32[]{:S(2)}) async-start(), calls=%async_computation.10 | async-start | bytes 1327104 | tf_op jit(solution)/shard_map/reduce_scatter | solution.py:250
  377.5 241.5 %reduce-scatter.17.cloned.1.call-start = ((), (), s32[]{:S(2)}) async-start(), calls=%async_computation.12 | async-start | bytes 5308416 | tf_op jit(solution)/shard_map/reduce_scatter | solution.py:268
  384.6 333.0 %reduce-scatter.15.cloned.1.call-start = ((), (), s32[]{:S(2)}) async-start(), calls=%async_computation.11 | async-start | bytes 5308416 | tf_op jit(solution)/shard_map/reduce_scatter | solution.py:262
  392.7 406.1 %all-reduce.14.cloned.1.call-start = ((), (), s32[]{:S(2)}) async-start(), calls=%async_computation.14 | async-start | bytes 3833856 | tf_op jit(solution)/shard_map/psum | solution.py:296
  394.7 328.8 %copy-start.35 = (bf16[768]{0:T(1024)(128)(2,1)S(1)}, bf16[768]{0:T(1024)(128)(2,1)}, u32[]{:S(2)}) copy-start(bf16[768]{0:T(1024)(128)(2,1)} %get-tuple-element.285) | copy-start | bytes 4612
  394.7 328.8 %copy-start.36 = (bf16[768]{0:T(1024)(128)(2,1)S(1)}, bf16[768]{0:T(1024)(128)(2,1)}, u32[]{:S(2)}) copy-start(bf16[768]{0:T(1024)(128)(2,1)} %get-tuple-element.353) | copy-start | bytes 4612
  397.8 395.7 %copy-start.32 = (f32[512]{0:T(512)S(1)}, f32[512]{0:T(512)}, u32[]{:S(2)}) copy-start(f32[512]{0:T(512)} %copy-done.31) | copy-start | bytes 6148
  (50 other events, 204.5 us)
Sparse Core Ops, SparseCore 0:
  18.3 31.6 all-gather.2
  52.1 28.9 all-gather.4
  284.3 37.9 reduce-scatter.8
  324.8 37.9 reduce-scatter.10
  374.3 79.1 reduce-scatter.18
  457.4 63.6 reduce-scatter.12
  524.7 94.1 reduce-scatter.16
  622.6 95.0 reduce-scatter.14
  720.8 48.9 all-reduce.13
where the time goes:
time: 818 us; the launch traced here: 814 us
  waiting for transfers between devices  442 us (54%)
  matrix products  153 us (19%)
  local copies, waits for them, and re-layouts  85.8 us (10%)
  other arithmetic  67.2 us (8%)
  blocking collectives  48.7 us (6%)
  between operations  15.7 us (2%)
    reduce_scatter x1, waiting for transfers between devices, body(): lax.psum_scatter(grad_w_inner.astype(jnp.bfloat16), 'dp', scatter_dimensi...  98.7 us
    reduce_scatter x1, waiting for transfers between devices, body(): lax.psum_scatter(grad_w_outer.astype(jnp.bfloat16), 'dp', scatter_dimensi...  97.9 us
    reduce_scatter x1, waiting for transfers between devices, body(): lax.psum_scatter(grad_w_attn_out.astype(jnp.bfloat16), 'dp', scatter_dime...  65.4 us
    unnamed x10, waiting for transfers between devices  56.4 us
    reduce_scatter x1, waiting for transfers between devices, body(): lax.psum_scatter(value_part.astype(jnp.bfloat16), 'seq', scatter_dimensio...  40.5 us
    unnamed x1, blocking collectives  37.2 us
    reduce_scatter x1, waiting for transfers between devices, body(): lax.psum_scatter(key_part.astype(jnp.bfloat16), 'seq', scatter_dimension=...  35.2 us
    all_gather x1, waiting for transfers between devices, body(): lax.all_gather(key_rows, 'seq', axis=1, tiled=True)  31.1 us
  transfers between devices with their start and end apart: 9, of which 8 were waited for; matrix products, arithmetic and copies ran while one was open for 9% of the time, Pallas kernels for 0%

commit v1 on v0

v1 whole, which is shorter than its diff:
```python
import functools
import math

import jax
import jax.numpy as jnp
from jax import lax
from jax.experimental import pallas as pl
from jax.experimental.pallas import tpu as pltpu
from jax.sharding import PartitionSpec as P

LOW = jnp.bfloat16
F32 = jnp.float32
HEADS = 12
HEAD_DIM = 64
LANES = 128
VMEM = 56 * 1024 * 1024
MASKED = -1e30
EPS = 1e-12
HALF_ROOT = math.sqrt(0.5)
PHI_SCALE = 1.0 / math.sqrt(2.0 * math.pi)


def dot(left, right):
    return jnp.dot(left, right, preferred_element_type=F32)


def dot_nt(left, right):
    return lax.dot_general(left, right, (((1,), (1,)), ((), ())), preferred_element_type=F32)


def dot_tn(left, right):
    return lax.dot_general(left, right, (((0,), (0,)), ((), ())), preferred_element_type=F32)


def turned(block):
    return block.astype(F32).T.astype(LOW)


def head_lanes(rows, head):
    lane = lax.broadcasted_iota(jnp.int32, (rows, LANES), 1)
    return (lane >= HEAD_DIM) if head else (lane < HEAD_DIM)


def spread(column, width):
    return jnp.concatenate([column] * (width // LANES), axis=1)


def attend_kernel(need, q_ref, k_ref, v_ref, segk_ref, segq_ref, o_ref, ot_ref, lse_ref,
                  qt, vt, km, mx, tot, acc, *, block, count):
    tokens = block * count
    for i in range(count):
        rows = pl.ds(i * block, block)
        qt[:, rows] = turned(q_ref[rows, :])
        vt[:, rows] = turned(v_ref[rows, :])
    for h in range(2):
        km[h] = jnp.where(head_lanes(tokens, h), k_ref[...], jnp.zeros((), LOW))

    def over_queries(qb, carry):
        cols = pl.ds(pl.multiple_of(qb * block, block), block)
        mx[...] = jnp.full(mx.shape, MASKED, F32)
        tot[...] = jnp.zeros(tot.shape, F32)
        acc[...] = jnp.zeros(acc.shape, F32)

        def over_keys(kb, carry):
            @pl.when(need[qb * count + kb] > 0)
            def _():
                rows = pl.ds(pl.multiple_of(kb * block, block), block)
                same = spread(segk_ref[rows, :], block) == segq_ref[0:1, cols]
                qtb = qt[:, cols]
                for h in range(2):
                    half = pl.ds(h * HEAD_DIM, HEAD_DIM)
                    s = dot(km[h, rows, :], qtb)
                    s = jnp.where(same, s, MASKED)
                    m_old = mx[h : h + 1, :]
                    m_new = jnp.maximum(m_old, jnp.max(s, axis=0, keepdims=True))
                    p = jnp.exp(s - m_new)
                    alpha = jnp.exp(m_old - m_new)
                    mx[h : h + 1, :] = m_new
                    tot[h : h + 1, :] = alpha * tot[h : h + 1, :] + jnp.sum(p, axis=0, keepdims=True)
                    acc[half, :] = alpha * acc[half, :] + dot(vt[half, rows], p.astype(LOW))
            return carry

        lax.fori_loop(0, count, over_keys, 0)
        total = tot[0:2, :]
        inv = 1.0 / total
        full = jnp.concatenate(
            [acc[0:HEAD_DIM, :] * inv[0:1, :], acc[HEAD_DIM:, :] * inv[1:2, :]], axis=0
        )
        ot_ref[:, cols] = full.astype(LOW)
        o_ref[cols, :] = full.T.astype(LOW)
        lse_ref[0, 0:2, cols] = mx[0:2, :] + jnp.log(total)
        return carry

    lax.fori_loop(0, count, over_queries, 0)


def attend(packed, seg_col, seg_row, need, pairs, block):
    tokens = packed.shape[0]
    count = tokens // block
    width = pairs * LANES
    return pl.pallas_call(
        functools.partial(attend_kernel, block=block, count=count),
        grid_spec=pltpu.PrefetchScalarGridSpec(
            num_scalar_prefetch=1,
            grid=(pairs,),
            in_specs=[
                pl.BlockSpec((tokens, LANES), lambda j, n: (0, j)),
                pl.BlockSpec((tokens, LANES), lambda j, n: (0, j + pairs)),
                pl.BlockSpec((tokens, LANES), lambda j, n: (0, j + 2 * pairs)),
                pl.BlockSpec((tokens, LANES), lambda j, n: (0, 0)),
                pl.BlockSpec((8, tokens), lambda j, n: (0, 0)),
            ],
            out_specs=[
                pl.BlockSpec((tokens, LANES), lambda j, n: (0, j)),
                pl.BlockSpec((LANES, tokens), lambda j, n: (j, 0)),
                pl.BlockSpec((1, 8, tokens), lambda j, n: (j, 0, 0)),
            ],
            scratch_shapes=[
                pltpu.VMEM((LANES, tokens), LOW),
                pltpu.VMEM((LANES, tokens), LOW),
                pltpu.VMEM((2, tokens, LANES), LOW),
                pltpu.VMEM((8, block), F32),
                pltpu.VMEM((8, block), F32),
                pltpu.VMEM((LANES, block), F32),
            ],
        ),
        out_shape=[
            jax.ShapeDtypeStruct((tokens, width), LOW),
            jax.ShapeDtypeStruct((width, tokens), LOW),
            jax.ShapeDtypeStruct((pairs, 8, tokens), F32),
        ],
        compiler_params=pltpu.CompilerParams(vmem_limit_bytes=VMEM),
        cost_estimate=pl.CostEstimate(flops=2 * tokens * tokens * width * 2, bytes_accessed=8 * tokens * width, transcendentals=tokens * tokens * 2 * pairs),
        name="attend",
    )(need, packed, packed, packed, seg_col, seg_row)


def attend_back_kernel(need, q_ref, k_ref, v_ref, do_ref, ot_ref, lse_ref, segk_ref, segq_ref,
                       dq_ref, dk_ref, dv_ref, qt, dot_t, kt, km, vm, qm, dom, cen, dqt, dk, dv,
                       *, block, count):
    tokens = block * count
    zero = jnp.zeros((), LOW)
    for i in range(count):
        rows = pl.ds(i * block, block)
        qt[:, rows] = turned(q_ref[rows, :])
        kt[:, rows] = turned(k_ref[rows, :])
        do_t = do_ref[rows, :].astype(F32).T
        dot_t[:, rows] = do_t.astype(LOW)
        both = do_t * ot_ref[:, rows].astype(F32)
        cen[0:1, rows] = jnp.sum(both[0:HEAD_DIM, :], axis=0, keepdims=True)
        cen[1:2, rows] = jnp.sum(both[HEAD_DIM:, :], axis=0, keepdims=True)
    for h in range(2):
        lanes = head_lanes(tokens, h)
        km[h] = jnp.where(lanes, k_ref[...], zero)
        vm[h] = jnp.where(lanes, v_ref[...], zero)
        qm[h] = jnp.where(lanes, q_ref[...], zero)
        dom[h] = jnp.where(lanes, do_ref[...], zero)
    dqt[...] = jnp.zeros(dqt.shape, F32)
    dk[...] = jnp.zeros(dk.shape, F32)
    dv[...] = jnp.zeros(dv.shape, F32)

    def over_queries(qb, carry):
        cols = pl.ds(pl.multiple_of(qb * block, block), block)

        def over_keys(kb, carry):
            @pl.when(need[qb * count + kb] > 0)
            def _():
                rows = pl.ds(pl.multiple_of(kb * block, block), block)
                same = spread(segk_ref[rows, :], block) == segq_ref[0:1, cols]
                qtb = qt[:, cols]
                dob = dot_t[:, cols]
                dk_add = jnp.zeros((block, LANES), F32)
                dv_add = jnp.zeros((block, LANES), F32)
                for h in range(2):
                    half = pl.ds(h * HEAD_DIM, HEAD_DIM)
                    s = dot(km[h, rows, :], qtb)
                    s = jnp.where(same, s, MASKED)
                    p = jnp.exp(s - lse_ref[0, h : h + 1, cols])
                    dp = dot(vm[h, rows, :], dob)
                    ds = (p * (dp - cen[h : h + 1, cols])).astype(LOW)
                    dv_add += dot(p.astype(LOW), dom[h, cols, :])
                    dk_add += dot(ds, qm[h, cols, :])
                    dqt[half, cols] += dot(kt[half, rows], ds)
                dv[rows, :] += dv_add
                dk[rows, :] += dk_add
            return carry

        lax.fori_loop(0, count, over_keys, 0)
        return carry

    lax.fori_loop(0, count, over_queries, 0)
    dk_ref[...] = dk[...].astype(LOW)
    dv_ref[...] = dv[...].astype(LOW)
    for i in range(count):
        rows = pl.ds(i * block, block)
        dq_ref[rows, :] = (dqt[:, rows].T * HEAD_DIM ** (-0.5)).astype(LOW)


def attend_back(packed, grads, ot, lse, seg_col, seg_row, need, pairs, block):
    tokens = packed.shape[0]
    count = tokens // block
    width = pairs * LANES
    return pl.pallas_call(
        functools.partial(attend_back_kernel, block=block, count=count),
        grid_spec=pltpu.PrefetchScalarGridSpec(
            num_scalar_prefetch=1,
            grid=(pairs,),
            in_specs=[
                pl.BlockSpec((tokens, LANES), lambda j, n: (0, j)),
                pl.BlockSpec((tokens, LANES), lambda j, n: (0, j + pairs)),
                pl.BlockSpec((tokens, LANES), lambda j, n: (0, j + 2 * pairs)),
                pl.BlockSpec((tokens, LANES), lambda j, n: (0, j)),
                pl.BlockSpec((LANES, tokens), lambda j, n: (j, 0)),
                pl.BlockSpec((1, 8, tokens), lambda j, n: (j, 0, 0)),
                pl.BlockSpec((tokens, LANES), lambda j, n: (0, 0)),
                pl.BlockSpec((8, tokens), lambda j, n: (0, 0)),
            ],
            out_specs=[pl.BlockSpec((tokens, LANES), lambda j, n: (0, j))] * 3,
            scratch_shapes=[
                pltpu.VMEM((LANES, tokens), LOW),
                pltpu.VMEM((LANES, tokens), LOW),
                pltpu.VMEM((LANES, tokens), LOW),
                pltpu.VMEM((2, tokens, LANES), LOW),
                pltpu.VMEM((2, tokens, LANES), LOW),
                pltpu.VMEM((2, tokens, LANES), LOW),
                pltpu.VMEM((2, tokens, LANES), LOW),
                pltpu.VMEM((8, tokens), F32),
                pltpu.VMEM((LANES, tokens), F32),
                pltpu.VMEM((tokens, LANES), F32),
                pltpu.VMEM((tokens, LANES), F32),
            ],
        ),
        out_shape=[jax.ShapeDtypeStruct((tokens, width), LOW)] * 3,
        compiler_params=pltpu.CompilerParams(vmem_limit_bytes=VMEM),
        cost_estimate=pl.CostEstimate(flops=2 * tokens * tokens * width * 5, bytes_accessed=20 * tokens * width, transcendentals=tokens * tokens * 2 * pairs),
        name="attend_back",
    )(need, packed, packed, packed, grads, ot, lse, seg_col, seg_row)


def row_mean(values):
    return jnp.mean(values, axis=-1, keepdims=True)


def normal(values):
    centre = values - row_mean(values)
    scale = lax.rsqrt(row_mean(centre * centre) + EPS)
    return centre * scale, scale


def normal_back(hat, scale, grads):
    return scale * (grads - row_mean(grads) - hat * row_mean(grads * hat))


def column_total(values):
    return jnp.sum(values, axis=0, keepdims=True)


def feed_kernel(x_ref, o_ref, wa_ref, ba_ref, ga_ref, sa_ref, wi_ref, bi_ref, wo_ref, bo_ref,
                gf_ref, sf_ref, go_ref, seg_ref,
                g_ref, gp_ref, yl_ref, yt_ref, hat_ref, scale_ref, out_ref, dh_ref, dz_ref, dzt_ref,
                small_ref, pool_ref, yl, acc):
    step = pl.program_id(0)

    @pl.when(step == 0)
    def _():
        h1 = x_ref[...].astype(F32) + dot(o_ref[...], wa_ref[...]) + ba_ref[...].astype(F32)
        hat, scale = normal(h1)
        y1 = hat * ga_ref[...].astype(F32) + sa_ref[...].astype(F32)
        hat_ref[...] = hat
        scale_ref[...] = jnp.broadcast_to(scale, scale_ref.shape)
        y1_low = y1.astype(LOW)
        yl[...] = y1_low
        yl_ref[...] = y1_low
        yt_ref[...] = y1.T.astype(LOW)
        acc[...] = y1 + bo_ref[...].astype(F32)

    u = dot(yl[...], wi_ref[...]) + bi_ref[...].astype(F32)
    cdf = 0.5 * (1.0 + lax.erf(u * HALF_ROOT))
    g = (u * cdf).astype(LOW)
    g_ref[...] = g
    gp_ref[...] = (cdf + u * (PHI_SCALE * jnp.exp(-0.5 * u * u))).astype(LOW)
    acc[...] += dot(g, wo_ref[...])

    @pl.when(step == pl.num_programs(0) - 1)
    def _():
        hat, scale = normal(acc[...])
        gain = gf_ref[...].astype(F32)
        out = hat * gain + sf_ref[...].astype(F32)
        out_ref[...] = out
        dy = go_ref[...].astype(F32)
        dh = normal_back(hat, scale, dy * gain)
        dh_ref[...] = dh
        dz = dh.astype(LOW)
        dz_ref[...] = dz
        dzt_ref[...] = dh.T.astype(LOW)
        small_ref[...] = jnp.zeros(small_ref.shape, F32)
        small_ref[0:1, :] = column_total(dy * hat)
        small_ref[1:2, :] = column_total(dy)
        small_ref[2:3, :] = column_total(dz.astype(F32))
        slots = pool_ref.shape[0]
        tokens = out.shape[0]
        place = lax.broadcasted_iota(jnp.int32, (slots, tokens), 0)
        onehot = (place == seg_ref[0:1, :]).astype(LOW)
        high = out.astype(LOW)
        rest = (out - high.astype(F32)).astype(LOW)
        pool_ref[...] = dot(onehot, high) + dot(onehot, rest)


def feed(x, o, wa, ba, ga, sa, wi, bi, wo, bo, gf, sf, go, seg_row, slots, block):
    tokens, dim = x.shape
    wide = wi.shape[1]
    whole = lambda a: pl.BlockSpec(a.shape, lambda i: (0,) * a.ndim)
    vec = lambda a: a.reshape(1, -1)
    ins = (x, o, wa, vec(ba), vec(ga), vec(sa), wi, vec(bi), wo, vec(bo), vec(gf), vec(sf), go, seg_row)
    specs = [whole(a) for a in ins]
    specs[6] = pl.BlockSpec((dim, block), lambda i: (0, i))
    specs[7] = pl.BlockSpec((1, block), lambda i: (0, i))
    specs[8] = pl.BlockSpec((block, dim), lambda i: (i, 0))
    outs = [
        ((tokens, wide), LOW, (tokens, block), lambda i: (0, i)),
        ((tokens, wide), LOW, (tokens, block), lambda i: (0, i)),
        ((tokens, dim), LOW, None, None),
        ((dim, tokens), LOW, None, None),
        ((tokens, dim), F32, None, None),
        ((tokens, LANES), F32, None, None),
        ((tokens, dim), F32, None, None),
        ((tokens, dim), F32, None, None),
        ((tokens, dim), LOW, None, None),
        ((dim, tokens), LOW, None, None),
        ((8, dim), F32, None, None),
        ((slots, dim), F32, None, None),
    ]
    return pl.pallas_call(
        feed_kernel,
        grid=(wide // block,),
        in_specs=specs,
        out_specs=[
            pl.BlockSpec(b or s, m or (lambda i: (0, 0))) for s, _, b, m in outs
        ],
        out_shape=[jax.ShapeDtypeStruct(s, t) for s, t, _, _ in outs],
        scratch_shapes=[pltpu.VMEM((tokens, dim), LOW), pltpu.VMEM((tokens, dim), F32)],
        compiler_params=pltpu.CompilerParams(vmem_limit_bytes=VMEM),
        cost_estimate=pl.CostEstimate(flops=4 * tokens * dim * wide + 2 * tokens * dim * dim, bytes_accessed=4 * dim * wide + 4 * tokens * wide + 30 * tokens * dim, transcendentals=2 * tokens * wide),
        name="feed",
    )(*ins)


def outer_kernel(dzt_ref, g_ref, out_ref):
    out_ref[0] = dot(dzt_ref[...], g_ref[...]).astype(LOW)


def outer_grads(dzt, g, block):
    dim, tokens = dzt.shape
    wide = g.shape[1]
    count = wide // block
    return pl.pallas_call(
        outer_kernel,
        grid=(count,),
        in_specs=[
            pl.BlockSpec((dim, tokens), lambda i: (0, 0)),
            pl.BlockSpec((tokens, block), lambda i: (0, i)),
        ],
        out_specs=pl.BlockSpec((1, dim, block), lambda i: (i, 0, 0)),
        out_shape=jax.ShapeDtypeStruct((count, dim, block), LOW),
        compiler_params=pltpu.CompilerParams(vmem_limit_bytes=VMEM),
        cost_estimate=pl.CostEstimate(flops=2 * tokens * dim * wide, bytes_accessed=2 * dim * wide + 2 * tokens * (wide + dim), transcendentals=0),
        name="outer_grads",
    )(dzt, g)


def inner_kernel(dz_ref, gp_ref, yt_ref, wo_ref, wi_ref, dh_ref, hat_ref, scale_ref, ga_ref, wa_ref,
                 grad_ref, bias_ref, dsum_ref, da_ref, do_ref, small_ref, acc):
    step = pl.program_id(0)

    @pl.when(step == 0)
    def _():
        acc[...] = dh_ref[...]

    du = (dot_nt(dz_ref[...], wo_ref[...]) * gp_ref[...].astype(F32)).astype(LOW)
    grad_ref[0] = dot(yt_ref[...], du).astype(LOW)
    bias_ref[...] = column_total(du.astype(F32))
    acc[...] += dot_nt(du, wi_ref[...])

    @pl.when(step == pl.num_programs(0) - 1)
    def _():
        hat = hat_ref[...]
        dy = acc[...]
        dh = normal_back(hat, scale_ref[:, 0:1], dy * ga_ref[...].astype(F32))
        dsum_ref[...] = dh
        da = dh.astype(LOW)
        da_ref[...] = da
        do_ref[...] = dot_nt(da, wa_ref[...]).astype(LOW)
        small_ref[...] = jnp.zeros(small_ref.shape, F32)
        small_ref[0:1, :] = column_total(dy * hat)
        small_ref[1:2, :] = column_total(dy)
        small_ref[2:3, :] = column_total(da.astype(F32))


def inner_grads(dz, gp, yt, wo, wi, dh, hat, scale, ga, wa, block):
    tokens, dim = dz.shape
    wide = wi.shape[1]
    count = wide // block
    whole = lambda a: pl.BlockSpec(a.shape, lambda i: (0,) * a.ndim)
    ins = (dz, gp, yt, wo, wi, dh, hat, scale, ga.reshape(1, -1), wa)
    specs = [whole(a) for a in ins]
    specs[1] = pl.BlockSpec((tokens, block), lambda i: (0, i))
    specs[3] = pl.BlockSpec((block, dim), lambda i: (i, 0))
    specs[4] = pl.BlockSpec((dim, block), lambda i: (0, i))
    outs = [
        ((count, dim, block), LOW, (1, dim, block), lambda i: (i, 0, 0)),
        ((1, wide), F32, (1, block), lambda i: (0, i)),
        ((tokens, dim), F32, None, None),
        ((tokens, dim), LOW, None, None),
        ((tokens, dim), LOW, None, None),
        ((8, dim), F32, None, None),
    ]
    return pl.pallas_call(
        inner_kernel,
        grid=(count,),
        in_specs=specs,
        out_specs=[pl.BlockSpec(b or s, m or (lambda i: (0, 0))) for s, _, b, m in outs],
        out_shape=[jax.ShapeDtypeStruct(s, t) for s, t, _, _ in outs],
        scratch_shapes=[pltpu.VMEM((tokens, dim), F32)],
        compiler_params=pltpu.CompilerParams(vmem_limit_bytes=VMEM),
        cost_estimate=pl.CostEstimate(flops=6 * tokens * dim * wide + 2 * tokens * dim * dim, bytes_accessed=6 * dim * wide + 2 * tokens * wide + 24 * tokens * dim, transcendentals=0),
        name="inner_grads",
    )(*ins)


def swap(values, name, mask):
    size = lax.axis_size(name)
    return lax.ppermute(values, name, [(i, i ^ mask) for i in range(size)])


def bit_masks(size):
    return [1 << b for b in range(size.bit_length() - 1)]


def total_of(parts, index, axis):
    picked = [lax.dynamic_slice_in_dim(p, index, 1, axis) for p in parts]
    return sum(p.astype(F32) for p in picked)


def halve(parts, name, mask, axis):
    bit = (lax.axis_index(name) // mask) % 2
    sent = total_of(parts, 1 - bit, axis).astype(LOW)
    got = swap(sent, name, mask)
    kept = [lax.dynamic_slice_in_dim(p, bit, 1, axis) for p in parts]
    return kept + [got]


def add_up(parts):
    return sum(p.astype(F32) for p in parts)


def both_sides(piece, name, mask, axis):
    got = swap(piece, name, mask)
    bit = (lax.axis_index(name) // mask) % 2
    first = jnp.where(bit == 0, piece, got)
    second = jnp.where(bit == 0, got, piece)
    return jnp.concatenate([first, second], axis=axis)


def split_bits(size):
    return (2,) * (size.bit_length() - 1)


def reduce_whole(grads, order, n_dp, n_seq):
    tail = grads.shape[2:]
    dp_bits, seq_bits = len(split_bits(n_dp)), len(split_bits(n_seq))
    parts = [grads.reshape(split_bits(n_dp) + split_bits(n_seq) + tail)]
    done = []
    for name, mask in order:
        bit = mask.bit_length() - 1
        axis = dp_bits - 1 - bit if name == "dp" else dp_bits + seq_bits - 1 - bit
        parts = halve(parts, name, mask, axis)
        if name == "seq":
            done.append((mask, axis))
    piece = add_up(parts).astype(LOW)
    for mask, axis in sorted(done, reverse=True):
        piece = both_sides(piece, "seq", mask, axis)
    return piece.reshape((piece.size // (tail[0] * tail[1]),) + tail)


def body(hidden_in, passage_lengths, w_qkv, b_query, b_value, w_attn_out, b_attn_out, gain_attn,
         bias_attn, w_inner, b_inner, w_outer, b_outer, gain_ffn, bias_ffn, grad_out):
    rows, chunk, dim = hidden_in.shape
    n_dp, n_seq = lax.axis_size("dp"), lax.axis_size("seq")
    wide = w_inner.shape[1]
    slots = passage_lengths.shape[1]
    group = n_seq // rows
    seq = lax.axis_index("seq")
    side, member = seq // group, seq % group
    mine = rows * chunk
    tokens = group * mine
    heads = HEADS // group
    cols = heads * HEAD_DIM
    pairs = (heads + 1) // 2
    padded = pairs * LANES
    block = 256
    row_at = lambda a, d: lax.dynamic_index_in_dim(a, side ^ d, 0, keepdims=False)
    head_cols = lambda a, m, start, axis: lax.dynamic_slice_in_dim(a, start + m * cols, cols, axis)
    widen = lambda a: jnp.pad(a, ((0, 0),) * (a.ndim - 1) + ((0, padded - cols),)) if padded > cols else a

    hidden = jnp.concatenate(
        [row_at(hidden_in, 0)] + [swap(row_at(hidden_in, d), "seq", d * group) for d in range(1, rows)], axis=0
    )
    cotangent = jnp.concatenate(
        [row_at(grad_out, 0)] + [swap(row_at(grad_out, d), "seq", d * group) for d in range(1, rows)], axis=0
    )
    hidden_all = jnp.concatenate([hidden] + [swap(hidden, "seq", e) for e in range(1, group)], axis=0)
    start = jnp.concatenate(
        [((side ^ d) * group + (member ^ e)) * chunk + jnp.arange(chunk, dtype=jnp.int32)
         for e in range(group) for d in range(rows)]
    )
    ends = jnp.cumsum(row_at(passage_lengths, 0), dtype=jnp.int32)
    segs = jnp.sum((start[:, None] >= ends[None, :]).astype(jnp.int32), axis=1, dtype=jnp.int32)
    seg_col = jnp.broadcast_to(segs[:, None], (tokens, LANES))
    seg_row = jnp.broadcast_to(segs[None, :], (8, tokens))
    per_block = segs.reshape(tokens // block, block)
    low_seg, high_seg = jnp.min(per_block, axis=1), jnp.max(per_block, axis=1)
    need = (
        jnp.maximum(low_seg[:, None], low_seg[None, :]) <= jnp.minimum(high_seg[:, None], high_seg[None, :])
    ).astype(jnp.int32).reshape(-1)

    scale = HEAD_DIM ** (-0.5)
    three = lambda m: [head_cols(w_qkv, m, i * dim, 1) for i in range(3)]
    w_q, w_k, w_v = three(member)
    w_local = jnp.concatenate([widen(w_q * scale), widen(w_k), widen(w_v)], axis=1)
    b_local = jnp.concatenate(
        [widen(head_cols(b_query, member, 0, 0) * scale), jnp.zeros((padded,), LOW), widen(head_cols(b_value, member, 0, 0))]
    )
    packed = (dot(hidden_all, w_local) + b_local.astype(F32)).astype(LOW)
    o_local, o_turned, lse = attend(packed, seg_col, seg_row, need, pairs, block)

    def to_columns(parts):
        whole = jnp.zeros((mine, dim), LOW)
        for e, part in enumerate(parts):
            whole = lax.dynamic_update_slice_in_dim(whole, part, (member ^ e) * cols, 1)
        return whole

    def by_member(local):
        split = local.reshape(group, mine, -1)
        return [split[0]] + [swap(split[e], "seq", e) for e in range(1, group)]

    o_full = to_columns([p[:, :cols] for p in by_member(o_local)])
    seg_mine = seg_row[:, :mine]
    (g_low, g_slope, y1_low, y1_turned, hat, hat_scale, out_mine, dh2, dz, dz_turned, small_two, pool) = feed(
        hidden, o_full, w_attn_out, b_attn_out, gain_attn, bias_attn, w_inner, b_inner, w_outer,
        b_outer, gain_ffn, bias_ffn, cotangent, seg_mine, slots, 768)

    for e in bit_masks(group):
        pool = pool + swap(pool, "seq", e)
    pool = pool.astype(LOW)

    def place(own, others):
        stack = jnp.zeros((rows,) + own.shape, F32)
        stack = lax.dynamic_update_index_in_dim(stack, own.astype(F32), side, 0)
        for d, other in enumerate(others, 1):
            stack = lax.dynamic_update_index_in_dim(stack, other.astype(F32), side ^ d, 0)
        return stack

    out_got = [swap(jnp.concatenate([out_mine[d * chunk:(d + 1) * chunk].astype(LOW), pool]), "seq", d * group)
               for d in range(1, rows)]
    out = place(out_mine[:chunk], [a[:chunk] for a in out_got])
    sums = place(pool, [a[chunk:] for a in out_got])
    pooled = sums / jnp.maximum(passage_lengths.astype(F32), 1.0)[:, :, None]

    seq_masks, dp_masks = bit_masks(n_seq), bit_masks(n_dp)
    member_masks = [("seq", m) for m in seq_masks if m < group]
    side_masks = [("seq", m) for m in seq_masks if m >= group]
    dp_stages = [("dp", m) for m in dp_masks]

    grad_outer = outer_grads(dz_turned, g_low, 384)
    outer_parts = grad_outer.reshape(grad_outer.shape[0], dim, -1)
    if outer_parts.shape[0] != n_dp:
        outer_parts = outer_parts.transpose(0, 2, 1).reshape(n_dp, wide // n_dp, dim).transpose(0, 2, 1)
    sum_outer = reduce_whole(
        outer_parts.reshape(n_dp, n_seq, dim // n_seq, wide // n_dp),
        member_masks + dp_stages[1:2] + dp_stages[:1] + side_masks + dp_stages[2:], n_dp, n_seq)
    grad_w_outer = sum_outer.reshape(dim, wide // n_dp).T.astype(F32)

    grad_inner, bias_inner, dh1, da, do_full, small_one = inner_grads(
        dz, g_slope, y1_turned, w_outer, w_inner, dh2, hat, hat_scale, gain_attn, w_attn_out, 768)
    if grad_inner.shape[0] != n_seq:
        grad_inner = grad_inner.transpose(1, 0, 2).reshape(dim, n_seq, wide // n_seq).transpose(1, 0, 2)
    inner_parts = grad_inner.reshape(n_seq, n_dp, dim // n_dp, wide // n_seq).transpose(1, 0, 2, 3)
    sum_inner = reduce_whole(inner_parts, member_masks + dp_stages[:1] + side_masks + dp_stages[1:], n_dp, n_seq)
    grad_w_inner = sum_inner.transpose(1, 0, 2).reshape(dim // n_dp, wide).astype(F32)

    do_parts = [head_cols(do_full, member ^ e, 0, 1) for e in range(group)]
    do_local = jnp.concatenate([do_parts[0]] + [swap(do_parts[e], "seq", e) for e in range(1, group)], axis=0)

    grad_attn_out = dot_tn(o_full, da).astype(LOW)
    sizes = [wide] + [dim] * 6
    vectors = jnp.concatenate(
        [v.reshape(n_dp, -1) for v in (bias_inner, small_two[0], small_two[1], small_two[2], small_one[0], small_one[1], small_one[2])],
        axis=1)
    unit = dim // n_seq
    lines = -(-vectors.shape[1] // dim)
    vectors = jnp.pad(vectors, ((0, 0), (0, lines * dim - vectors.shape[1])))
    vectors = vectors.reshape(n_dp, lines, n_seq, unit).transpose(0, 2, 1, 3).astype(LOW)
    share = dim // n_dp
    attn_parts = grad_attn_out.reshape(n_dp, share, n_seq, unit).transpose(0, 2, 1, 3)
    fill = jnp.zeros((n_dp, n_seq, -lines % 8, unit), LOW)
    sum_attn = reduce_whole(
        jnp.concatenate([attn_parts, vectors, fill], axis=2),
        member_masks + side_masks + dp_stages, n_dp, n_seq)
    grad_w_attn_out = sum_attn[:, :share].transpose(1, 0, 2).reshape(share, dim).astype(F32)
    flat = sum_attn[:, share:share + lines].transpose(1, 0, 2).reshape(-1).astype(F32)
    pieces, at = [], 0
    for size in sizes:
        pieces.append(flat[at:at + size // n_dp])
        at += size // n_dp
    (grad_b_inner, grad_gain_ffn, grad_bias_ffn, grad_b_outer, grad_gain_attn, grad_bias_attn, grad_b_attn_out) = pieces

    d_query, d_key, d_value = attend_back(
        packed, widen(do_local), o_turned, lse, seg_col, seg_row, need, pairs, block)
    d_local = jnp.concatenate([a[:, :cols] for a in (d_query, d_key, d_value)], axis=1)
    grad_qkv = dot_tn(hidden_all, d_local).astype(LOW)

    def spread_bias(values):
        local = jnp.sum(values[:, :cols].astype(F32), axis=0)
        return lax.dynamic_update_slice_in_dim(jnp.zeros((dim,), F32), local, member * cols, 0)

    biases = jnp.concatenate(
        [spread_bias(d_query).reshape(n_dp, share), spread_bias(d_value).reshape(n_dp, share)], axis=1).astype(LOW)
    part = share // rows
    extra = LANES
    need_rows = -(-biases.shape[1] // extra)
    biases = jnp.pad(biases, ((0, 0), (0, rows * part * extra - biases.shape[1]))).reshape(n_dp, rows, part, extra)
    qkv_parts = jnp.concatenate([grad_qkv.reshape(n_dp, rows, part, 3 * cols), biases], axis=3)

    def reduce_group(grads, order):
        tail = grads.shape[2:]
        dp_bits, side_bits = len(split_bits(n_dp)), len(split_bits(rows))
        parts = [grads.reshape(split_bits(n_dp) + split_bits(rows) + tail)]
        done = []
        for name, mask in order:
            bit = mask.bit_length() - 1
            if name == "dp":
                axis = dp_bits - 1 - bit
            else:
                axis = dp_bits + side_bits - 1 - (bit - group.bit_length() + 1)
                done.append((mask, axis))
            parts = halve(parts, name, mask, axis)
        piece = add_up(parts).astype(LOW)
        for mask, axis in sorted(done, reverse=True):
            piece = both_sides(piece, "seq", mask, axis)
        return piece.reshape((rows,) + tail)

    sum_qkv = reduce_group(qkv_parts, dp_stages[:1] + side_masks + dp_stages[1:]).reshape(share, 3 * cols + extra)
    everyone = [sum_qkv] + [swap(sum_qkv, "seq", e) for e in range(1, group)]
    grad_w_qkv = jnp.zeros((share, 3 * dim), F32)
    bias_sum = 0.0
    ordered = jnp.zeros((group,) + sum_qkv.shape, LOW)
    for e, got in enumerate(everyone):
        ordered = lax.dynamic_update_index_in_dim(ordered, got, member ^ e, 0)
    ordered = ordered.astype(F32)
    grad_w_qkv = jnp.concatenate(
        [ordered[m, :, i * cols:(i + 1) * cols] for i in range(3) for m in range(group)], axis=1)
    bias_sum = sum(ordered[m, :, 3 * cols:] for m in range(group)).reshape(-1)
    grad_b_query, grad_b_value = bias_sum[:share], bias_sum[share:2 * share]

    d_parts = d_local.reshape(group, mine, 3 * cols)
    d_mine = [d_parts[0]] + [swap(d_parts[e], "seq", e) for e in range(1, group)]
    grad_hidden = dh1
    for e, part_e in enumerate(d_mine):
        w_e = jnp.concatenate(three(member ^ e), axis=1)
        grad_hidden = grad_hidden + dot_nt(part_e, w_e)
    in_got = [swap(grad_hidden[d * chunk:(d + 1) * chunk].astype(LOW), "seq", d * group) for d in range(1, rows)]
    grad_in = place(grad_hidden[:chunk], in_got)

    return (out, pooled, grad_in, grad_w_qkv, grad_b_query, grad_b_value, grad_w_attn_out,
            grad_b_attn_out, grad_gain_attn, grad_bias_attn, grad_w_inner, grad_b_inner,
            grad_w_outer, grad_b_outer, grad_gain_ffn, grad_bias_ffn)


def solution(mesh):
    tokens, rows, whole = P("dp", "seq", None), P("dp", None), P()
    vector, cube = P("dp"), P("dp", None, None)
    return jax.shard_map(
        body,
        mesh=mesh,
        in_specs=(tokens, rows) + (whole,) * 13 + (tokens,),
        out_specs=(tokens, cube, tokens, rows, vector, vector, rows, vector, vector, vector, rows,
                   vector, rows, vector, vector, vector),
        check_vma=False,
    )
```

time: 818 us -> 336 us (0.41)
  waiting for transfers between devices: 442 us -> 111 us
  matrix products: 153 us -> 17.4 us
  Pallas kernels: 0 us -> 92.9 us
  blocking collectives: 48.7 us -> 0 us
  local copies, waits for them, and re-layouts: 85.8 us -> 41.7 us
  starting transfers between devices: 0.71 us -> 31.5 us
  other arithmetic: 67.2 us -> 38.3 us
  between operations: 15.7 us -> 1.74 us
    reduce_scatter x5 -> x0, waiting for transfers between devices: 338 us -> none  [the longest x1 98.7 us: body(): lax.psum_scatter(grad_w_inner.astype(jnp.bfloat16), 'dp', scatter_dimensi...]
    dot_general x27 -> x5, matrix products: 153 us -> 17.4 us  [the longest x2 6.06 us: dot_nt(): lax.dot_general(left, right, (((1,), (1,)), ((), ())), preferred_element_...]
    ppermute x0 -> x36, waiting for transfers between devices: none -> 111 us  [swap(): return lax.ppermute(values, name, [(i, i ^ mask) for i in range(size)])]
    pallas_call x0 -> x5, Pallas kernels: none -> 92.9 us  [the longest x1 25.6 us: attend(): pl.pallas_call(functools.partial(attend_kernel, block=block, count=count)...]
    unnamed x10 -> x0, waiting for transfers between devices: 56.4 us -> none
    all_gather x2 -> x0, waiting for transfers between devices: 47.6 us -> none  [the longest x1 31.1 us: body(): lax.all_gather(key_rows, 'seq', axis=1, tiled=True)]
    unnamed x1 -> x0, blocking collectives: 37.2 us -> none
    ppermute x0 -> x36, starting transfers between devices: none -> 31.5 us  [swap(): return lax.ppermute(values, name, [(i, i ^ mask) for i in range(size)])]
  transfers between devices with their start and end apart: 9 -> 36, of which waited for: 8 -> 22; matrix products, arithmetic and copies ran while one was open for 9% -> 26% of each run, Pallas kernels for 0% -> 20%
where the time goes in v1:
time: 336 us; the launch traced here: 334 us
  waiting for transfers between devices  111 us (33%)
  Pallas kernels  92.9 us (28%)
  local copies, waits for them, and re-layouts  41.7 us (12%)
  other arithmetic  38.3 us (11%)
  starting transfers between devices  31.5 us (9%)
  matrix products  17.4 us (5%)
    ppermute x36, waiting for transfers between devices, swap(): return lax.ppermute(values, name, [(i, i ^ mask) for i in range(size)])  111 us
    ppermute x36, starting transfers between devices, swap(): return lax.ppermute(values, name, [(i, i ^ mask) for i in range(size)])  31.5 us
    pallas_call x1, Pallas kernels, attend(): pl.pallas_call(functools.partial(attend_kernel, block=block, count=count)...  25.6 us
    pallas_call x1, Pallas kernels, attend_back(): pl.pallas_call(functools.partial(attend_back_kernel, block=block, count=c...  24.8 us
    pallas_call x1, Pallas kernels, feed(): pl.pallas_call(feed_kernel, grid=(wide // block,), in_specs=specs, out_sp...  17.4 us
    convert_element_type x15, other arithmetic, halve(): sent = total_of(parts, 1 - bit, axis).astype(LOW)  17.2 us
    pallas_call x1, Pallas kernels, inner_grads(): pl.pallas_call(inner_kernel, grid=(count,), in_specs=specs, out_specs=[pl...  16.4 us
    pallas_call x1, Pallas kernels, outer_grads(): pl.pallas_call(outer_kernel, grid=(count,), in_specs=[pl.BlockSpec((dim,...  8.72 us
  transfers between devices with their start and end apart: 36, of which 22 were waited for; matrix products, arithmetic and copies ran while one was open for 26% of the time, Pallas kernels for 20%

profile of v1, /device:TPU:0, one launch (start us, length us, event | category | flops | bytes accessed | tf_op | source)
XLA Modules:
  0.0 334.3 jit_solution(17716227890709885109)
XLA Ops:
  8.1 8.0 %collective-permute-done = bf16[256,768]{1,0:T(8,128)(2,1)} collective-permute-done((bf16[256,768]{1,0:T(8,128)(2,1)}, bf16[256,768]{1,0:T(8,128)(2,1)}, u32[]{:S(2)}, u32[]{:S(2)}) %collective-permute-start) | collective-permute-done | bytes 393248 | tf_op jit(solution)/shard_map/ppermute | solution.py:432
  21.8 5.3 %add_convert_fusion.q_ref.k_ref.v_ref = bf16[1024,1152]{1,0:T(8,128)(2,1)} fusion(f32[1152]{0:T(1024)S(1)} %maximum_convert_fusion, bf16[768,384]{1,0:T(8,128)(2,1)S(1)} %get-tuple-element.123, bf16[768,384]{1,0:T(8,128)(2,1)S(1)} %get-tuple-element.124, bf16[768,384]{1,0:T(8,128)(2,1)S(1)} %get-tuple-element.125, ...), kind=kOutput, calls=%fused_computation | convolution fusion | flops 1824325632 | bytes 5706240 | tf_op jit(solution)/shard_map/dot_general | solution.py:24
  28.7 25.6 %attend.1 = (bf16[1024,384]{1,0:T(8,128)(2,1)}, bf16[384,1024]{1,0:T(8,128)(2,1)}, f32[3,8,1024]{2,1,0:T(8,128)}) custom-call(s32[16]{0:T(128)} %reshape.201.need, bf16[1024,1152]{1,0:T(8,128)(2,1)} %add_convert_fusion.q_ref.k_ref.v_ref, bf16[1024,1152]{1,0:T(8,128)(2,1)} %add_convert_fusion.q_ref.k_ref.v_ref, ...), custom_call_target="tpu_custom_call" | custom-call | flops 1610612736 | bytes 3145728 | tf_op jit(solution)/shard_map/attend/pallas_call | solution.py:101
  63.5 17.4 %feed.1 = (bf16[512,3072]{1,0:T(8,128)(2,1)}, bf16[512,3072]{1,0:T(8,128)(2,1)}, bf16[512,768]{1,0:T(8,128)(2,1)}, bf16[768,512]{1,0:T(8,128)(2,1)}, f32[512,768...) custom-call(bf16[512,768]{1,0:T(8,128)(2,1)} %pad_maximum_fusion.7.x, ...), custom_call_target="tpu_custom_call" | custom-call | flops 5435817984 | bytes 27525120 | tf_op jit(solution)/shard_map/feed/pallas_call | solution.py:333
  80.9 8.7 %outer_grads.1 = bf16[8,768,384]{2,1,0:T(8,128)(2,1)} custom-call(bf16[768,512]{1,0:T(8,128)(2,1)} %get-tuple-element.60.dzt_ref, bf16[512,3072]{1,0:T(8,128)(2,1)} %get-tuple-element.61.g_ref), custom_call_target="tpu_custom_call" | custom-call | flops 2415919104 | bytes 8650752 | tf_op jit(solution)/shard_map/outer_grads/pallas_call | solution.py:356
  89.7 3.3 constant_dynamic-slice_fusion.2
  93.1 16.4 %inner_grads.1 = (bf16[4,768,768]{2,1,0:T(8,128)(2,1)}, f32[1,3072]{1,0:T(1,128)}, f32[512,768]{1,0:T(8,128)}, bf16[512,768]{1,0:T(8,128)(2,1)}, bf16[512,768]{1,0:T(8,128)(2,1)}, /*index=5*/f32[8,768]{1,0:T(8,128)}) custom-call(bf16[512,768]{1,0:T(8,128)(2,1)} %get-tuple-element.42.dz_ref, bf16[512,3072]{1,0:T(8,128)(2,1)} %get-tuple-element.43.gp_ref, ...), custom_call_target="tpu_custom_call" | custom-call | flops 7851737088 | bytes 26738688 | tf_op jit(solution)/shard_map/inner_grads/pallas_call | solution.py:417
  109.6 3.3 constant_dynamic-slice_fusion
  116.9 3.5 %reshape.195 = bf16[8,96,4,192]{3,2,1,0:T(4,128)(2,1)S(1)} reshape(bf16[768,768]{1,0:T(8,128)(2,1)} %convolution_convert_fusion.1) | data formatting | bytes 2359296 | tf_op jit(solution)/shard_map/reshape | solution.py:604
  130.9 24.8 %attend_back.1 = (bf16[1024,384]{1,0:T(8,128)(2,1)}, bf16[1024,384]{1,0:T(8,128)(2,1)}, bf16[1024,384]{1,0:T(8,128)(2,1)}) custom-call(s32[16]{0:T(128)} %reshape.201.need, bf16[1024,1152]{1,0:T(8,128)(2,1)} %add_convert_fusion.q_ref.k_ref.v_ref, bf16[1024,1152]{1,0:T(8,128)(2,1)} %add_convert_fusion.q_ref.k_ref.v_ref, ...), custom_call_target="tpu_custom_call" | custom-call | flops 4026531840 | bytes 7864320 | tf_op jit(solution)/shard_map/attend_back/pallas_call | solution.py:203
  158.5 4.2 %convolution_convert_fusion = bf16[768,1152]{1,0:T(8,128)(2,1)S(1)} fusion(bf16[1024,1152]{1,0:T(8,128)(2,1)S(1)} %constant_dynamic-update-slice_fusion.4, bf16[512,768]{1,0:T(8,128)(2,1)} %collective-permute-done.1, bf16[256,768]{1,0:T(8,128)(2,1)} %collective-permute-done, bf16[256,768]{1,0:T(8,128)(2,1)S(1)} %copy-done.7), kind=kOutput, calls=%fused_computation.6 | convolution fusion | flops 1817542656 | bytes 5701632 | tf_op jit(solution)/shard_map/dot_general | solution.py:32
  165.3 8.8 %collective-permute-done.16 = bf16[2,2,2,1,1,104,192]{5,6,4,3,2,1,0:T(8,128)(2,1)S(1)} collective-permute-done((bf16[2,2,2,1,1,104,192]{5,6,4,3,2,1,0:T(8,128)(2,1)S(1)}, bf16[2,2,2,1,1,104,192]{5,6,4,3,2,1,0:T(8,128)(2,1)S(1)}, u32[]{:S(2)}, u32[]{:S(2)}) %collective-permute-start.16) | collective-permute-done | bytes 319520 | tf_op jit(solution)/shard_map/ppermute | solution.py:432
  174.9 9.5 %collective-permute-start.17 = (bf16[2,2,1,1,1,104,192]{5,6,4,3,2,1,0:T(8,128)(2,1)}, bf16[2,2,1,1,1,104,192]{5,6,4,3,2,1,0:T(8,128)(2,1)}, u32[]{:S(2)}, u32[]{:S(2)}) collective-permute-start(bf16[2,2,1,1,1,104,192]{5,6,4,3,2,1,0:T(8,128)(2,1)} %add_convert_fusion.10), channel_id=1, source_target_pairs={{0,4},{4,0},{8,12},{12,8},{16,20},{20,16},{24,28},{28,24},{1,5},{5... | collective-permute-start | bytes 479240 | tf_op jit(solution)/shard_map/ppermute | solution.py:432
  185.5 3.6 %collective-permute-done.17 = bf16[2,2,1,1,1,104,192]{5,6,4,3,2,1,0:T(8,128)(2,1)} collective-permute-done((bf16[2,2,1,1,1,104,192]{5,6,4,3,2,1,0:T(8,128)(2,1)}, bf16[2,2,1,1,1,104,192]{5,6,4,3,2,1,0:T(8,128)(2,1)}, u32[]{:S(2)}, u32[]{:S(2)}) %collective-permute-start.17) | collective-permute-done | bytes 159776 | tf_op jit(solution)/shard_map/ppermute | solution.py:432
  207.8 8.4 %collective-permute-done.9 = bf16[2,2,1,2,48,1280]{5,4,3,2,1,0:T(8,128)(2,1)} collective-permute-done((bf16[2,2,1,2,48,1280]{5,4,3,2,1,0:T(8,128)(2,1)}, bf16[2,2,1,2,48,1280]{5,4,3,2,1,0:T(8,128)(2,1)}, u32[]{:S(2)}, u32[]{:S(2)}) %collective-permute-start.9) | collective-permute-done | bytes 983072 | tf_op jit(solution)/shard_map/ppermute | solution.py:432
  221.1 3.7 %add_add_fusion = f32[512,768]{1,0:T(8,128)S(1)} fusion(f32[512,768]{1,0:T(8,128)} %get-tuple-element.48, f32[512,768]{1,0:T(8,128)} %fusion, bf16[512,1152]{1,0:T(8,128)(2,1)} %collective-permute-done.7, bf16[768,384]{1,0:T(8,128)(2,1)S(1)} %copy-done.16, bf16[768,384]{1,0:T(8,128)(2,1)} %get-tuple-element.128, bf16[768,384]{1,0:T(8,128)(2,1)S(1)} %copy-done.15), kind=kOutput, calls=%fused_computation.26 | convolution fusion | flops 912064512 | bytes 7667712 | tf_op jit(solution)/shard_map/dot_general | solution.py:28
  226.0 6.5 %collective-permute-done.10 = bf16[2,2,1,1,48,1280]{5,4,3,2,1,0:T(8,128)(2,1)} collective-permute-done((bf16[2,2,1,1,48,1280]{5,4,3,2,1,0:T(8,128)(2,1)}, bf16[2,2,1,1,48,1280]{5,4,3,2,1,0:T(8,128)(2,1)}, u32[]{:S(2)}, u32[]{:S(2)}) %collective-permute-start.10) | collective-permute-done | bytes 491552 | tf_op jit(solution)/shard_map/ppermute | solution.py:432
  234.7 6.0 %collective-permute-done.11 = bf16[2,1,1,1,48,1280]{5,4,3,2,1,0:T(8,128)(2,1)S(1)} collective-permute-done((bf16[2,1,1,1,48,1280]{5,4,3,2,1,0:T(8,128)(2,1)S(1)}, bf16[2,1,1,1,48,1280]{5,4,3,2,1,0:T(8,128)(2,1)S(1)}, u32[]{:S(2)}, u32[]{:S(2)}) %collective-permute-start.11) | collective-permute-done | bytes 245792 | tf_op jit(solution)/shard_map/ppermute | solution.py:432
  241.9 6.8 %collective-permute-done.12 = bf16[1,1,1,1,48,1280]{5,4,3,2,1,0:T(8,128)(2,1)S(1)} collective-permute-done((bf16[1,1,1,1,48,1280]{5,4,3,2,1,0:T(8,128)(2,1)S(1)}, bf16[1,1,1,1,48,1280]{5,4,3,2,1,0:T(8,128)(2,1)S(1)}, u32[]{:S(2)}, u32[]{:S(2)}) %collective-permute-start.12) | collective-permute-done | bytes 122912 | tf_op jit(solution)/shard_map/ppermute | solution.py:432
  258.0 14.4 %collective-permute-done.30 = bf16[2,1,2,2,1,192,384]{6,5,4,3,2,1,0:T(8,128)(2,1)S(1)} collective-permute-done((bf16[2,1,2,2,1,192,384]{6,5,4,3,2,1,0:T(8,128)(2,1)S(1)}, bf16[2,1,2,2,1,192,384]{6,5,4,3,2,1,0:T(8,128)(2,1)S(1)}, u32[]{:S(2)}, u32[]{:S(2)}) %collective-permute-start.30) | collective-permute-done | bytes 1179680 | tf_op jit(solution)/shard_map/ppermute | solution.py:432
  274.9 10.5 %collective-permute-done.23 = bf16[2,2,1,2,1,96,768]{6,5,2,1,0,4,3:T(8,128)(2,1)S(1)} collective-permute-done((bf16[2,2,1,2,1,96,768]{6,5,2,1,0,4,3:T(8,128)(2,1)S(1)}, bf16[2,2,1,2,1,96,768]{6,5,2,1,0,4,3:T(8,128)(2,1)S(1)}, u32[]{:S(2)}, u32[]{:S(2)}) %collective-permute-start.23) | collective-permute-done | bytes 1179680 | tf_op jit(solution)/shard_map/ppermute | solution.py:432
  287.9 9.7 %collective-permute-done.31 = bf16[2,1,1,2,1,192,384]{6,5,4,3,2,1,0:T(8,128)(2,1)S(1)} collective-permute-done((bf16[2,1,1,2,1,192,384]{6,5,4,3,2,1,0:T(8,128)(2,1)S(1)}, bf16[2,1,1,2,1,192,384]{6,5,4,3,2,1,0:T(8,128)(2,1)S(1)}, u32[]{:S(2)}, u32[]{:S(2)}) %collective-permute-start.31) | collective-permute-done | bytes 589856 | tf_op jit(solution)/shard_map/ppermute | solution.py:432
  302.7 4.9 %collective-permute-done.32 = bf16[2,1,1,1,1,192,384]{6,5,4,3,2,1,0:T(8,128)(2,1)S(1)} collective-permute-done((bf16[2,1,1,1,1,192,384]{6,5,4,3,2,1,0:T(8,128)(2,1)S(1)}, bf16[2,1,1,1,1,192,384]{6,5,4,3,2,1,0:T(8,128)(2,1)S(1)}, u32[]{:S(2)}, u32[]{:S(2)}) %collective-permute-start.32) | collective-permute-done | bytes 294944 | tf_op jit(solution)/shard_map/ppermute | solution.py:432
  313.2 7.1 %collective-permute-done.33 = bf16[1,1,1,1,1,192,384]{6,5,4,3,2,1,0:T(8,128)(2,1)S(1)} collective-permute-done((bf16[1,1,1,1,1,192,384]{6,5,4,3,2,1,0:T(8,128)(2,1)S(1)}, bf16[1,1,1,1,1,192,384]{6,5,4,3,2,1,0:T(8,128)(2,1)S(1)}, u32[]{:S(2)}, u32[]{:S(2)}) %collective-permute-start.33) | collective-permute-done | bytes 147488 | tf_op jit(solution)/shard_map/ppermute | solution.py:432
  (296 shorter events, 112.4 us)
Async XLA Ops:
  2.9 13.2 %collective-permute-start = (bf16[256,768]{1,0:T(8,128)(2,1)}, bf16[256,768]{1,0:T(8,128)(2,1)}, u32[]{:S(2)}, u32[]{:S(2)}) collective-permute-start(bf16[256,768]{1,0:T(8,128)(2,1)} %get-tuple-element.136), channel_id=1, source_target_pairs={{0,2},{1,3},{2,0},{3,1},{4,6},{5,7},{6,4},{7,5},{8,10},{9,11},{10,... | collective-permute-start | bytes 1179656 | tf_op jit(solution)/shard_map/ppermute | solution.py:432
  7.9 52.7 %collective-permute-start.3 = (bf16[256,768]{1,0:T(8,128)(2,1)}, bf16[256,768]{1,0:T(8,128)(2,1)}, u32[]{:S(2)}, u32[]{:S(2)}) collective-permute-start(bf16[256,768]{1,0:T(8,128)(2,1)} %get-tuple-element.132), channel_id=1, source_target_pairs={{0,2},{1,3},{2,0},{3,1},{4,6},{5,7},{6,4},{7,5},{8,10},{9,11},{10,... | collective-permute-start | bytes 1179656 | tf_op jit(solution)/shard_map/ppermute | solution.py:432
  55.8 6.8 %collective-permute-start.2 = (bf16[512,384]{1,0:T(8,128)(2,1)S(1)}, bf16[512,384]{1,0:T(8,128)(2,1)S(1)}, u32[]{:S(2)}, u32[]{:S(2)}) collective-permute-start(bf16[512,384]{1,0:T(8,128)(2,1)S(1)} %get-tuple-element.133), channel_id=1, source_target_pairs={{0,1},{1,0},{2,3},{3,2},{4,5},{5,4},{6,7},{7,6},{8,9},{9,8},{10,11... | collective-permute-start | bytes 1179656 | tf_op jit(solution)/shard_map/ppermute | solution.py:432
  93.0 158.0 %collective-permute-start.29 = (bf16[2,2,2,2,1,192,384]{6,5,4,3,2,1,0:T(8,128)(2,1)}, bf16[2,2,2,2,1,192,384]{6,5,4,3,2,1,0:T(8,128)(2,1)}, u32[]{:S(2)}, u32[]{:S(2)}) collective-permute-start(bf16[2,2,2,2,1,192,384]{6,5,4,3,2,1,0:T(8,128)(2,1)} %constant_dynamic-slice_fusion.2), channel_id=1, source_target_pairs={{0,1},{1,0},{2,3},{3,2},{4,5},{5,4},{6,7},{7,6},{8,9},{9,8},{10,11... | collective-permute-start | bytes 7077896 | tf_op jit(solution)/shard_map/ppermute | solution.py:432
  112.9 142.0 %collective-permute-start.22 = (bf16[2,2,2,2,1,96,768]{6,5,2,1,0,4,3:T(8,128)(2,1)}, bf16[2,2,2,2,1,96,768]{6,5,2,1,0,4,3:T(8,128)(2,1)}, u32[]{:S(2)}, u32[]{:S(2)}) collective-permute-start(bf16[2,2,2,2,1,96,768]{6,5,2,1,0,4,3:T(8,128)(2,1)} %constant_dynamic-slice_fusion), channel_id=1, source_target_pairs={{0,1},{1,0},{2,3},{3,2},{4,5},{5,4},{6,7},{7,6},{8,9},{9,8},{10,11... | collective-permute-start | bytes 7077896 | tf_op jit(solution)/shard_map/ppermute | solution.py:432
  125.2 37.4 %collective-permute-start.15 = (bf16[2,2,2,2,1,104,192]{5,6,4,3,2,1,0:T(8,128)(2,1)S(1)}, bf16[2,2,2,2,1,104,192]{5,6,4,3,2,1,0:T(8,128)(2,1)S(1)}, u32[]{:S(2)}, u32[]{:S(2)}) collective-permute-start(bf16[2,2,2,2,1,104,192]{5,6,4,3,2,1,0:T(8,128)(2,1)S(1)} %constant_dynamic-slice_fusion.1), channel_id=1, source_target_pairs={{0,1},{1,0},{2,3},{3,2},{4,5},{5,4},{6,7},{7,6},{8,9},{9,8},{10,11... | collective-permute-start | bytes 1916936 | tf_op jit(solution)/shard_map/ppermute | solution.py:432
  130.0 65.7 %collective-permute-start.5 = (bf16[264,768]{1,0:T(8,128)(2,1)}, bf16[264,768]{1,0:T(8,128)(2,1)}, u32[]{:S(2)}, u32[]{:S(2)}) collective-permute-start(bf16[264,768]{1,0:T(8,128)(2,1)} %pad_maximum_fusion.14), channel_id=1, source_target_pairs={{0,2},{1,3},{2,0},{3,1},{4,6},{5,7},{6,4},{7,5},{8,10},{9,11},{10,... | collective-permute-start | bytes 1216520 | tf_op jit(solution)/shard_map/ppermute | solution.py:432
  162.8 11.3 %collective-permute-start.16 = (bf16[2,2,2,1,1,104,192]{5,6,4,3,2,1,0:T(8,128)(2,1)S(1)}, bf16[2,2,2,1,1,104,192]{5,6,4,3,2,1,0:T(8,128)(2,1)S(1)}, u32[]{:S(2)}, u32[]{:S(2)}) collective-permute-start(bf16[2,2,2,1,1,104,192]{5,6,4,3,2,1,0:T(8,128)(2,1)S(1)} %add_convert_fusion.6), channel_id=1, source_target_pairs={{0,2},{1,3},{2,0},{3,1},{4,6},{5,7},{6,4},{7,5},{8,10},{9,11},{10,... | collective-permute-start | bytes 958472 | tf_op jit(solution)/shard_map/ppermute | solution.py:432
  174.9 14.2 %collective-permute-start.17 = (bf16[2,2,1,1,1,104,192]{5,6,4,3,2,1,0:T(8,128)(2,1)}, bf16[2,2,1,1,1,104,192]{5,6,4,3,2,1,0:T(8,128)(2,1)}, u32[]{:S(2)}, u32[]{:S(2)}) collective-permute-start(bf16[2,2,1,1,1,104,192]{5,6,4,3,2,1,0:T(8,128)(2,1)} %add_convert_fusion.10), channel_id=1, source_target_pairs={{0,4},{4,0},{8,12},{12,8},{16,20},{20,16},{24,28},{28,24},{1,5},{5... | collective-permute-start | bytes 479240 | tf_op jit(solution)/shard_map/ppermute | solution.py:432
  194.1 22.1 %collective-permute-start.9 = (bf16[2,2,1,2,48,1280]{5,4,3,2,1,0:T(8,128)(2,1)}, bf16[2,2,1,2,48,1280]{5,4,3,2,1,0:T(8,128)(2,1)}, u32[]{:S(2)}, u32[]{:S(2)}) collective-permute-start(bf16[2,2,1,2,48,1280]{5,4,3,2,1,0:T(8,128)(2,1)} %fusion.12), channel_id=1, source_target_pairs={{0,4},{4,0},{8,12},{12,8},{16,20},{20,16},{24,28},{28,24},{1,5},{5... | collective-permute-start | bytes 2949128 | tf_op jit(solution)/shard_map/ppermute | solution.py:432
  194.8 26.3 %collective-permute-start.7 = (bf16[512,1152]{1,0:T(8,128)(2,1)}, bf16[512,1152]{1,0:T(8,128)(2,1)}, u32[]{:S(2)}, u32[]{:S(2)}) collective-permute-start(bf16[512,1152]{1,0:T(8,128)(2,1)} %slice.161), channel_id=1, source_target_pairs={{0,1},{1,0},{2,3},{3,2},{4,5},{5,4},{6,7},{7,6},{8,9},{9,8},{10,11... | collective-permute-start | bytes 3538952 | tf_op jit(solution)/shard_map/ppermute | solution.py:432
  218.1 14.5 %collective-permute-start.10 = (bf16[2,2,1,1,48,1280]{5,4,3,2,1,0:T(8,128)(2,1)}, bf16[2,2,1,1,48,1280]{5,4,3,2,1,0:T(8,128)(2,1)}, u32[]{:S(2)}, u32[]{:S(2)}) collective-permute-start(bf16[2,2,1,1,48,1280]{5,4,3,2,1,0:T(8,128)(2,1)} %add_convert_fusion.5), channel_id=1, source_target_pairs={{0,2},{1,3},{2,0},{3,1},{4,6},{5,7},{6,4},{7,5},{8,10},{9,11},{10,... | collective-permute-start | bytes 1474568 | tf_op jit(solution)/shard_map/ppermute | solution.py:432
  224.9 16.9 %collective-permute-start.8 = (bf16[256,768]{1,0:T(8,128)(2,1)S(1)}, bf16[256,768]{1,0:T(8,128)(2,1)S(1)}, u32[]{:S(2)}, u32[]{:S(2)}) collective-permute-start(bf16[256,768]{1,0:T(8,128)(2,1)S(1)} %slice.234), channel_id=1, source_target_pairs={{0,2},{1,3},{2,0},{3,1},{4,6},{5,7},{6,4},{7,5},{8,10},{9,11},{10,... | collective-permute-start | bytes 1179656 | tf_op jit(solution)/shard_map/ppermute | solution.py:432
  233.9 6.8 %collective-permute-start.11 = (bf16[2,1,1,1,48,1280]{5,4,3,2,1,0:T(8,128)(2,1)S(1)}, bf16[2,1,1,1,48,1280]{5,4,3,2,1,0:T(8,128)(2,1)S(1)}, u32[]{:S(2)}, u32[]{:S(2)}) collective-permute-start(bf16[2,1,1,1,48,1280]{5,4,3,2,1,0:T(8,128)(2,1)S(1)} %add_convert_fusion.9), channel_id=1, source_target_pairs={{0,8},{4,12},{8,0},{12,4},{16,24},{20,28},{24,16},{28,20},{1,9},{5... | collective-permute-start | bytes 737288 | tf_op jit(solution)/shard_map/ppermute | solution.py:432
  241.7 7.0 %collective-permute-start.12 = (bf16[1,1,1,1,48,1280]{5,4,3,2,1,0:T(8,128)(2,1)S(1)}, bf16[1,1,1,1,48,1280]{5,4,3,2,1,0:T(8,128)(2,1)S(1)}, u32[]{:S(2)}, u32[]{:S(2)}) collective-permute-start(bf16[1,1,1,1,48,1280]{5,4,3,2,1,0:T(8,128)(2,1)S(1)} %add_convert_fusion.16), channel_id=1, source_target_pairs={{0,16},{4,20},{8,24},{12,28},{16,0},{20,4},{24,8},{28,12},{1,17},{... | collective-permute-start | bytes 368648 | tf_op jit(solution)/shard_map/ppermute | solution.py:432
  252.6 19.7 %collective-permute-start.30 = (bf16[2,1,2,2,1,192,384]{6,5,4,3,2,1,0:T(8,128)(2,1)S(1)}, bf16[2,1,2,2,1,192,384]{6,5,4,3,2,1,0:T(8,128)(2,1)S(1)}, u32[]{:S(2)}, u32[]{:S(2)}) collective-permute-start(bf16[2,1,2,2,1,192,384]{6,5,4,3,2,1,0:T(8,128)(2,1)S(1)} %add_convert_fusion.1), channel_id=1, source_target_pairs={{0,8},{4,12},{8,0},{12,4},{16,24},{20,28},{24,16},{28,20},{1,9},{5... | collective-permute-start | bytes 3538952 | tf_op jit(solution)/shard_map/ppermute | solution.py:432
  256.5 28.8 %collective-permute-start.23 = (bf16[2,2,1,2,1,96,768]{6,5,2,1,0,4,3:T(8,128)(2,1)S(1)}, bf16[2,2,1,2,1,96,768]{6,5,2,1,0,4,3:T(8,128)(2,1)S(1)}, u32[]{:S(2)}, u32[]{:S(2)}) collective-permute-start(bf16[2,2,1,2,1,96,768]{6,5,2,1,0,4,3:T(8,128)(2,1)S(1)} %add_convert_fusion.2), channel_id=1, source_target_pairs={{0,4},{4,0},{8,12},{12,8},{16,20},{20,16},{24,28},{28,24},{1,5},{5... | collective-permute-start | bytes 3538952 | tf_op jit(solution)/shard_map/ppermute | solution.py:432
  273.6 23.9 %collective-permute-start.31 = (bf16[2,1,1,2,1,192,384]{6,5,4,3,2,1,0:T(8,128)(2,1)S(1)}, bf16[2,1,1,2,1,192,384]{6,5,4,3,2,1,0:T(8,128)(2,1)S(1)}, u32[]{:S(2)}, u32[]{:S(2)}) collective-permute-start(bf16[2,1,1,2,1,192,384]{6,5,4,3,2,1,0:T(8,128)(2,1)S(1)} %add_convert_fusion.3), channel_id=1, source_target_pairs={{0,4},{4,0},{8,12},{12,8},{16,20},{20,16},{24,28},{28,24},{1,5},{5... | collective-permute-start | bytes 1769480 | tf_op jit(solution)/shard_map/ppermute | solution.py:432
  286.6 14.7 %collective-permute-start.24 = (bf16[2,2,1,1,1,96,768]{6,5,2,1,0,4,3:T(8,128)(2,1)S(1)}, bf16[2,2,1,1,1,96,768]{6,5,2,1,0,4,3:T(8,128)(2,1)S(1)}, u32[]{:S(2)}, u32[]{:S(2)}) collective-permute-start(bf16[2,2,1,1,1,96,768]{6,5,2,1,0,4,3:T(8,128)(2,1)S(1)} %add_convert_fusion.4), channel_id=1, source_target_pairs={{0,2},{1,3},{2,0},{3,1},{4,6},{5,7},{6,4},{7,5},{8,10},{9,11},{10,... | collective-permute-start | bytes 1769480 | tf_op jit(solution)/shard_map/ppermute | solution.py:432
  298.7 8.8 %collective-permute-start.32 = (bf16[2,1,1,1,1,192,384]{6,5,4,3,2,1,0:T(8,128)(2,1)S(1)}, bf16[2,1,1,1,1,192,384]{6,5,4,3,2,1,0:T(8,128)(2,1)S(1)}, u32[]{:S(2)}, u32[]{:S(2)}) collective-permute-start(bf16[2,1,1,1,1,192,384]{6,5,4,3,2,1,0:T(8,128)(2,1)S(1)} %add_convert_fusion.7), channel_id=1, source_target_pairs={{0,2},{1,3},{2,0},{3,1},{4,6},{5,7},{6,4},{7,5},{8,10},{9,11},{10,... | collective-permute-start | bytes 884744 | tf_op jit(solution)/shard_map/ppermute | solution.py:432
  302.4 7.3 %collective-permute-start.25 = (bf16[2,1,1,1,1,96,768]{6,5,2,1,0,4,3:T(8,128)(2,1)S(1)}, bf16[2,1,1,1,1,96,768]{6,5,2,1,0,4,3:T(8,128)(2,1)S(1)}, u32[]{:S(2)}, u32[]{:S(2)}) collective-permute-start(bf16[2,1,1,1,1,96,768]{6,5,2,1,0,4,3:T(8,128)(2,1)S(1)} %add_convert_fusion.8), channel_id=1, source_target_pairs={{0,8},{4,12},{8,0},{12,4},{16,24},{20,28},{24,16},{28,20},{1,9},{5... | collective-permute-start | bytes 884744 | tf_op jit(solution)/shard_map/ppermute | solution.py:432
  308.5 11.7 %collective-permute-start.33 = (bf16[1,1,1,1,1,192,384]{6,5,4,3,2,1,0:T(8,128)(2,1)S(1)}, bf16[1,1,1,1,1,192,384]{6,5,4,3,2,1,0:T(8,128)(2,1)S(1)}, u32[]{:S(2)}, u32[]{:S(2)}) collective-permute-start(bf16[1,1,1,1,1,192,384]{6,5,4,3,2,1,0:T(8,128)(2,1)S(1)} %add_convert_fusion.12), channel_id=1, source_target_pairs={{0,16},{4,20},{8,24},{12,28},{16,0},{20,4},{24,8},{28,12},{1,17},{... | collective-permute-start | bytes 442376 | tf_op jit(solution)/shard_map/ppermute | solution.py:432
  310.8 12.5 %collective-permute-start.26 = (bf16[1,1,1,1,1,96,768]{6,5,2,1,0,4,3:T(8,128)(2,1)S(1)}, bf16[1,1,1,1,1,96,768]{6,5,2,1,0,4,3:T(8,128)(2,1)S(1)}, u32[]{:S(2)}, u32[]{:S(2)}) collective-permute-start(bf16[1,1,1,1,1,96,768]{6,5,2,1,0,4,3:T(8,128)(2,1)S(1)} %add_convert_fusion.14), channel_id=1, source_target_pairs={{0,16},{4,20},{8,24},{12,28},{16,0},{20,4},{24,8},{28,12},{1,17},{... | collective-permute-start | bytes 442376 | tf_op jit(solution)/shard_map/ppermute | solution.py:432
  324.4 5.8 %collective-permute-start.27 = (bf16[1,1,1,1,1,96,768]{6,5,2,1,0,4,3:T(8,128)(2,1)S(1)}, bf16[1,1,1,1,1,96,768]{6,5,2,1,0,4,3:T(8,128)(2,1)S(1)}, u32[]{:S(2)}, u32[]{:S(2)}) collective-permute-start(bf16[1,1,1,1,1,96,768]{6,5,2,1,0,4,3:T(8,128)(2,1)S(1)} %add_convert_fusion.13), channel_id=1, source_target_pairs={{0,2},{1,3},{2,0},{3,1},{4,6},{5,7},{6,4},{7,5},{8,10},{9,11},{10,... | collective-permute-start | bytes 442376 | tf_op jit(solution)/shard_map/ppermute | solution.py:432
  (58 other events, 420.0 us)
